TPU v7x, 128 devices: a whole 4x4x4 slice. The times are simulated.
128 devices in a mesh: rows: 32 (over y_hi, x, z), cols: 4 (over y_lo, core).
Axes of the slice: x: 4, y: 4 (y_hi: 2, y_lo: 2; y = y_hi * 2 + y_lo), z: 4, core: 2. Of those that a mesh axis runs over, the one named last changes fastest.
Arguments:
- noise: bfloat16 [2, 2, 4096, 8192], P(None, None, 'rows', 'cols'), may hold values from -6 to 6
- root_eigen: bfloat16 [2, 4096, 8192], P(None, 'rows', 'cols'), may hold values from 0.19921875 to 2
Outputs:
- field: float32 [2, 8192, 8192], P(None, ('rows', 'cols'))
All inputs are finite; a program needn't handle non-finite values.
Results may differ from a plain program's by a relative error of at most 0.0003.
Values sent between devices are 32-bit elements; how exact they have to be, the bound alone decides.
No kernel may reach another device: no remote copies, remote signals or barrier semaphores. Data moves between devices by JAX's collectives and lax.ppermute only.
A program may use at most 128 MiB of HBM per device.

v0:
```python
import jax
import jax.numpy as jnp
from jax import lax
from jax.sharding import PartitionSpec as P


def phase_pair(left_idx, right_idx, modulus):
    product = left_idx[:, None] * right_idx[None, :] % modulus
    phases = product.astype(jnp.float32) * (2.0 * jnp.pi / modulus)
    return (jnp.cos(phases), jnp.sin(phases))


def complex_table(left_idx, right_idx, modulus):
    cosine, sine = phase_pair(left_idx, right_idx, modulus)
    return jnp.stack([jnp.stack([cosine, sine], 1), jnp.stack([-sine, cosine], 1)], 0)


def contract(form, left, table):
    return jnp.einsum(
        form, left, table, precision=lax.Precision.HIGHEST, preferred_element_type=jnp.float32
    )


def split_sizes(length):
    outer_len = 2 ** ((length.bit_length() - 1) // 2)
    return (outer_len, length // outer_len)


def along_last(stacked):
    length = stacked.shape[-1]
    outer_len, inner_len = split_sizes(length)
    lead_dims = stacked.shape[1:-1]
    split = stacked.reshape((2,) + lead_dims + (outer_len, inner_len))
    outer_idx = jnp.arange(outer_len, dtype=jnp.int32)
    inner_idx = jnp.arange(inner_len, dtype=jnp.int32)
    step = contract("s...ab,satc->t...cb", split, complex_table(outer_idx, outer_idx, outer_len))
    cos_two, sin_two = phase_pair(outer_idx, inner_idx, length)
    turned = jnp.stack(
        [step[0] * cos_two - step[1] * sin_two, step[0] * sin_two + step[1] * cos_two]
    )
    final = contract("t...cb,tbud->u...dc", turned, complex_table(inner_idx, inner_idx, inner_len))
    return final.reshape((2,) + lead_dims + (length,))


def along_rows(stacked, scale_by):
    half_len = stacked.shape[2]
    outer_len, inner_len = split_sizes(half_len)
    dims_of = stacked.shape
    split = stacked.reshape(2, dims_of[1], outer_len, inner_len, dims_of[3])
    outer_idx = jnp.arange(outer_len, dtype=jnp.int32)
    inner_idx = jnp.arange(inner_len, dtype=jnp.int32)
    step = contract("spabv,satc->tpcbv", split, complex_table(outer_idx, outer_idx, outer_len))
    cos_two, sin_two = phase_pair(outer_idx, inner_idx, half_len)
    cos_two = cos_two[None, :, :, None]
    sin_two = sin_two[None, :, :, None]
    turned = jnp.stack(
        [step[0] * cos_two - step[1] * sin_two, step[0] * sin_two + step[1] * cos_two]
    )
    final = contract("tpcbv,tbud->pvudc", turned, complex_table(inner_idx, inner_idx, inner_len))
    return final.reshape(dims_of[1], dims_of[3], 2 * half_len) / scale_by


def one_block(noise_part, root_part):
    spectrum = noise_part.astype(jnp.float32) * root_part.astype(jnp.float32)[None]
    whole_cols = lax.all_to_all(spectrum, "cols", split_axis=2, concat_axis=3, tiled=True)
    length = whole_cols.shape[3]
    columns = along_last(whole_cols)
    full_rows = lax.all_to_all(columns, ("rows", "cols"), split_axis=3, concat_axis=2, tiled=True)
    half_len = full_rows.shape[2]
    mirror = jnp.concatenate([full_rows[:, :, :1], jnp.flip(full_rows[:, :, 1:], 2)], 2)
    part_re = full_rows[0]
    part_im = full_rows[1]
    sum_re = part_re + mirror[0]
    sum_im = part_im - mirror[1]
    diff_re = part_re - mirror[0]
    diff_im = part_im + mirror[1]
    theta = jnp.arange(half_len, dtype=jnp.int32).astype(jnp.float32) * (2.0 * jnp.pi / length)
    cos_row = jnp.cos(theta)[None, :, None]
    sin_row = jnp.sin(theta)[None, :, None]
    packed = jnp.stack(
        [
            sum_re - (cos_row * diff_im + sin_row * diff_re),
            sum_im + (cos_row * diff_re - sin_row * diff_im),
        ]
    )
    return along_rows(packed, length)


def shards(noise, root_eigen):

    def per_plane(plane_pair):
        return one_block(plane_pair[0][:, None], plane_pair[1][None])[0]

    return lax.map(per_plane, (jnp.swapaxes(noise, 0, 1), root_eigen))


def solution(mesh):
    return jax.shard_map(
        shards,
        mesh=mesh,
        in_specs=(P(None, None, "rows", "cols"), P(None, "rows", "cols")),
        out_specs=P(None, ("rows", "cols"), None),
        check_vma=False,
    )
```

profile of v0, /device:TPU:1, one launch (start us, length us, event | category | flops | bytes accessed | tf_op | source)
XLA Modules:
  0.0 464.5 jit_solution(2016120318165759494)
XLA Ops:
  0.0 5.2 %copy.74 = bf16[2,2,128,2048]{3,0,2,1:T(2,128)(2,1)} copy(bf16[2,2,128,2048]{3,2,1,0:T(8,128)(2,1)} %param.4) | data formatting | bytes 4194304 | tf_op args[0]
  5.2 458.4 %while.13 = (s32[]{:T(128)}, f32[2,64,8192]{2,1,0:T(8,128)}, bf16[2,2,128,2048]{3,1,2,0:T(2,128)(2,1)}, bf16[2,128,2048]{2,1,0:T(8,128)(2,1)S(1)}, s32[]{:T(128)}, /*index=5*/f32[]{:T(128)}) while((s32[]{:T(128)}, f32[2,64,8192]{2,1,0:T(8,128)}, bf16[2,2,128,2048]{3,1,2,0:T(2,128)(2,1)}, bf16[2,128,2048]{2,1,0:T(8,128)(2,1)S(1)}, s32[]{:T(128)}, ...), condition=%wide.region_1.2_spmd, body=%wide.region_0.1_spmd.sunk | while | flops 4038250496 | bytes 139689248 | solution.py:94
  32.8 5.0 %all-to-all-start = ((f32[2,1,128,2048]{3,0,1,2:T(2,128)}), f32[2,1,128,2048]{3,0,1,2:T(2,128)S(1)}, u32[]{:S(2)}, u32[]{:S(2)}) async-start(f32[2,1,128,2048]{3,0,1,2:T(2,128)} %convert_multiply_fusion.3), calls=%async_computation | async-start | bytes 4194304 | tf_op jit(solution)/shard_map/while/body/eval_jaxpr/all_to_all | solution.py:65
  39.5 23.2 %all-to-all-done = f32[2,1,128,2048]{3,0,1,2:T(2,128)S(1)} async-done(((f32[2,1,128,2048]{3,0,1,2:T(2,128)}), f32[2,1,128,2048]{3,0,1,2:T(2,128)S(1)}, u32[]{:S(2)}, u32[]{:S(2)}) %all-to-all-start) | async-done | bytes 2097184 | tf_op jit(solution)/shard_map/while/body/eval_jaxpr/all_to_all | solution.py:65
  72.4 6.4 %copy.89 = f32[2,1,32,128,64]{2,0,4,3,1:T(2,128)} copy(f32[2,1,32,128,64]{3,4,2,0,1:T(8,128)S(1)} %fusion.86) | data formatting | bytes 4194304 | tf_op jit(solution)/shard_map/while/body/eval_jaxpr/reshape | solution.py:42
  78.8 10.8 %reshape.469 = f32[128,1,4096]{2,1,0:T(1,128)} reshape(f32[8192,1,2,32]{3,2,1,0:T(2,128)} %bitcast.188) | data formatting | bytes 4194304 | tf_op jit(solution)/shard_map/while
  89.6 10.9 %all-to-all-start.1 = ((f32[128,1,4096]{2,1,0:T(1,128)}), f32[128,1,4096]{2,1,0:T(1,128)S(1)}, u32[]{:S(2)}, u32[]{:S(2)}) async-start(f32[128,1,4096]{2,1,0:T(1,128)} %reshape.469), calls=%async_computation.1 | async-start | bytes 4194304 | tf_op jit(solution)/shard_map/while/body/eval_jaxpr/all_to_all | solution.py:68
  100.8 30.0 %all-to-all-done.1 = f32[128,1,4096]{2,1,0:T(1,128)S(1)} async-done(((f32[128,1,4096]{2,1,0:T(1,128)}), f32[128,1,4096]{2,1,0:T(1,128)S(1)}, u32[]{:S(2)}, u32[]{:S(2)}) %all-to-all-start.1) | async-done | bytes 2097184 | tf_op jit(solution)/shard_map/while/body/eval_jaxpr/all_to_all | solution.py:68
  132.6 7.2 %reduce.2 = f32[128,4096]{1,0:T(8,128)S(1)} reduce(f32[128,1,4096]{2,1,0:T(1,128)} %copy-done.1, f32[]{:T(128)} %broadcast.702), dimensions={1}, to_apply=%all_to_all.48.reduce_sub_computation | reduce | bytes 4194308 | tf_op jit(solution)/shard_map/while/body/eval_jaxpr/all_to_all | solution.py:68
  139.9 8.5 %reshape.470 = f32[8192,1,2,32]{3,2,1,0:T(2,128)} reshape(f32[128,4096]{1,0:T(8,128)S(1)} %reduce.2) | data formatting | bytes 4194304 | tf_op jit(solution)/shard_map/while
  148.3 12.3 %copy.90 = f32[2,1,32,128,64]{4,3,2,0,1:T(8,128)} copy(f32[2,1,32,128,64]{2,0,4,3,1:T(2,128)} %bitcast.186) | data formatting | bytes 4194304 | tf_op jit(solution)/shard_map/while/body/eval_jaxpr/all_to_all | solution.py:68
  160.6 11.0 %copy.93 = f32[2,1,32,128,64]{4,2,3,0,1:T(8,128)} copy(f32[2,1,32,128,64]{2,0,4,3,1:T(2,128)} %bitcast.187) | data formatting | bytes 4194304 | tf_op jit(solution)/shard_map/while/body/eval_jaxpr/all_to_all | solution.py:68
  171.6 4.6 slice.132
  181.2 33.6 %rev.9 = f32[2,1,4095,64]{3,2,1,0:T(8,128)} reverse(f32[2,1,4095,64]{3,2,1,0:T(8,128)} %slice.132), dimensions={2} | reverse | bytes 4193280 | tf_op jit(solution)/shard_map/while/body/eval_jaxpr/jit(_flip)/rev | solution.py:70
  214.7 5.6 %fusion.89 = (f32[1,1,4096,64]{3,2,1,0:T(8,128)S(1)}, f32[1,1,4096,64]{3,2,1,0:T(8,128)S(1)}) fusion(f32[1,1,128,32,64]{4,3,2,1,0:T(8,128)S(1)} %copy.91, f32[4096]{0:T(1024)S(1)} %get-tuple-element.177, f32[4096]{0:T(1024)S(1)} %get-tuple-element.178, f32[1,1,128,32,64]{4,3,2,1,0:T(8,128)} %copy.92, f32[2,1,4095,64]{3,2,1,0:T(8,128)} %rev.9, ...), kind=kLoop, calls=%fused_computation.22.clone.1 | loop fusion | flops 4194304 | bytes 6324224 | tf_op jit(solution)/shard_map/while/body/eval_jaxpr/sub | solution.py:82
  229.1 9.0 %fusion.92 = f32[1,64,2,64,64]{1,3,4,2,0:T(8,128)} fusion(f32[2,64,64,64]{3,1,2,0:T(8,128)S(1)} %maximum_bitcast_fusion.35, f32[1,64,2,64]{1,3,0,2:T(8,128)S(1)} %get-tuple-element.170, f32[1,64,2,64]{1,3,0,2:T(8,128)S(1)} %get-tuple-element.171), kind=kOutput, calls=%fused_computation.8.clone.1 | convolution fusion | flops 805847040 | bytes 4259840 | tf_op jit(solution)/shard_map/while/body/eval_jaxpr/tpcbv,tbud->pvudc/dot_general | solution.py:19
  238.1 5.9 %copy.96 = f32[1,64,2,64,64]{4,3,2,1,0:T(8,128)} copy(f32[1,64,2,64,64]{1,3,4,2,0:T(8,128)} %fusion.92) | data formatting | bytes 4194304 | tf_op jit(solution)/shard_map/while/body/eval_jaxpr/div | solution.py:60
  252.9 4.8 %all-to-all-start = ((f32[2,1,128,2048]{3,0,1,2:T(2,128)}), f32[2,1,128,2048]{3,0,1,2:T(2,128)S(1)}, u32[]{:S(2)}, u32[]{:S(2)}) async-start(f32[2,1,128,2048]{3,0,1,2:T(2,128)} %convert_multiply_fusion.3), calls=%async_computation | async-start | bytes 4194304 | tf_op jit(solution)/shard_map/while/body/eval_jaxpr/all_to_all | solution.py:65
  259.4 23.2 %all-to-all-done = f32[2,1,128,2048]{3,0,1,2:T(2,128)S(1)} async-done(((f32[2,1,128,2048]{3,0,1,2:T(2,128)}), f32[2,1,128,2048]{3,0,1,2:T(2,128)S(1)}, u32[]{:S(2)}, u32[]{:S(2)}) %all-to-all-start) | async-done | bytes 2097184 | tf_op jit(solution)/shard_map/while/body/eval_jaxpr/all_to_all | solution.py:65
  292.3 6.4 %copy.89 = f32[2,1,32,128,64]{2,0,4,3,1:T(2,128)} copy(f32[2,1,32,128,64]{3,4,2,0,1:T(8,128)S(1)} %fusion.86) | data formatting | bytes 4194304 | tf_op jit(solution)/shard_map/while/body/eval_jaxpr/reshape | solution.py:42
  298.7 10.8 %reshape.469 = f32[128,1,4096]{2,1,0:T(1,128)} reshape(f32[8192,1,2,32]{3,2,1,0:T(2,128)} %bitcast.188) | data formatting | bytes 4194304 | tf_op jit(solution)/shard_map/while
  309.5 5.6 %all-to-all-start.1 = ((f32[128,1,4096]{2,1,0:T(1,128)}), f32[128,1,4096]{2,1,0:T(1,128)S(1)}, u32[]{:S(2)}, u32[]{:S(2)}) async-start(f32[128,1,4096]{2,1,0:T(1,128)} %reshape.469), calls=%async_computation.1 | async-start | bytes 4194304 | tf_op jit(solution)/shard_map/while/body/eval_jaxpr/all_to_all | solution.py:68
  315.3 30.0 %all-to-all-done.1 = f32[128,1,4096]{2,1,0:T(1,128)S(1)} async-done(((f32[128,1,4096]{2,1,0:T(1,128)}), f32[128,1,4096]{2,1,0:T(1,128)S(1)}, u32[]{:S(2)}, u32[]{:S(2)}) %all-to-all-start.1) | async-done | bytes 2097184 | tf_op jit(solution)/shard_map/while/body/eval_jaxpr/all_to_all | solution.py:68
  347.2 7.2 %reduce.2 = f32[128,4096]{1,0:T(8,128)S(1)} reduce(f32[128,1,4096]{2,1,0:T(1,128)} %copy-done.1, f32[]{:T(128)} %broadcast.702), dimensions={1}, to_apply=%all_to_all.48.reduce_sub_computation | reduce | bytes 4194308 | tf_op jit(solution)/shard_map/while/body/eval_jaxpr/all_to_all | solution.py:68
  354.4 8.5 %reshape.470 = f32[8192,1,2,32]{3,2,1,0:T(2,128)} reshape(f32[128,4096]{1,0:T(8,128)S(1)} %reduce.2) | data formatting | bytes 4194304 | tf_op jit(solution)/shard_map/while
  362.9 12.3 %copy.90 = f32[2,1,32,128,64]{4,3,2,0,1:T(8,128)} copy(f32[2,1,32,128,64]{2,0,4,3,1:T(2,128)} %bitcast.186) | data formatting | bytes 4194304 | tf_op jit(solution)/shard_map/while/body/eval_jaxpr/all_to_all | solution.py:68
  375.2 11.0 %copy.93 = f32[2,1,32,128,64]{4,2,3,0,1:T(8,128)} copy(f32[2,1,32,128,64]{2,0,4,3,1:T(2,128)} %bitcast.187) | data formatting | bytes 4194304 | tf_op jit(solution)/shard_map/while/body/eval_jaxpr/all_to_all | solution.py:68
  386.1 4.6 slice.132
  395.7 33.6 %rev.9 = f32[2,1,4095,64]{3,2,1,0:T(8,128)} reverse(f32[2,1,4095,64]{3,2,1,0:T(8,128)} %slice.132), dimensions={2} | reverse | bytes 4193280 | tf_op jit(solution)/shard_map/while/body/eval_jaxpr/jit(_flip)/rev | solution.py:70
  429.3 5.6 %fusion.89 = (f32[1,1,4096,64]{3,2,1,0:T(8,128)S(1)}, f32[1,1,4096,64]{3,2,1,0:T(8,128)S(1)}) fusion(f32[1,1,128,32,64]{4,3,2,1,0:T(8,128)S(1)} %copy.91, f32[4096]{0:T(1024)S(1)} %get-tuple-element.177, f32[4096]{0:T(1024)S(1)} %get-tuple-element.178, f32[1,1,128,32,64]{4,3,2,1,0:T(8,128)} %copy.92, f32[2,1,4095,64]{3,2,1,0:T(8,128)} %rev.9, ...), kind=kLoop, calls=%fused_computation.22.clone.1 | loop fusion | flops 4194304 | bytes 6324224 | tf_op jit(solution)/shard_map/while/body/eval_jaxpr/sub | solution.py:82
  443.7 9.0 %fusion.92 = f32[1,64,2,64,64]{1,3,4,2,0:T(8,128)} fusion(f32[2,64,64,64]{3,1,2,0:T(8,128)S(1)} %maximum_bitcast_fusion.35, f32[1,64,2,64]{1,3,0,2:T(8,128)S(1)} %get-tuple-element.170, f32[1,64,2,64]{1,3,0,2:T(8,128)S(1)} %get-tuple-element.171), kind=kOutput, calls=%fused_computation.8.clone.1 | convolution fusion | flops 805847040 | bytes 4259840 | tf_op jit(solution)/shard_map/while/body/eval_jaxpr/tpcbv,tbud->pvudc/dot_general | solution.py:19
  452.7 5.9 %copy.96 = f32[1,64,2,64,64]{4,3,2,1,0:T(8,128)} copy(f32[1,64,2,64,64]{1,3,4,2,0:T(8,128)} %fusion.92) | data formatting | bytes 4194304 | tf_op jit(solution)/shard_map/while/body/eval_jaxpr/div | solution.py:60
  (75 shorter events, 72.0 us)
Async XLA Ops:
  0.0 5.2 %copy-start.2 = (bf16[2,128,2048]{2,1,0:T(8,128)(2,1)S(1)}, bf16[2,128,2048]{2,1,0:T(8,128)(2,1)}, u32[]{:S(2)}) copy-start(bf16[2,128,2048]{2,1,0:T(8,128)(2,1)} %param.5) | copy-start | bytes 3145732
  32.8 29.8 %all-to-all-start = ((f32[2,1,128,2048]{3,0,1,2:T(2,128)}), f32[2,1,128,2048]{3,0,1,2:T(2,128)S(1)}, u32[]{:S(2)}, u32[]{:S(2)}) async-start(f32[2,1,128,2048]{3,0,1,2:T(2,128)} %convert_multiply_fusion.3), calls=%async_computation | async-start | bytes 4194304 | tf_op jit(solution)/shard_map/while/body/eval_jaxpr/all_to_all | solution.py:65
  68.1 2.0 copy-start.3
  68.1 2.0 copy-start.4
  89.6 41.2 %all-to-all-start.1 = ((f32[128,1,4096]{2,1,0:T(1,128)}), f32[128,1,4096]{2,1,0:T(1,128)S(1)}, u32[]{:S(2)}, u32[]{:S(2)}) async-start(f32[128,1,4096]{2,1,0:T(1,128)} %reshape.469), calls=%async_computation.1 | async-start | bytes 4194304 | tf_op jit(solution)/shard_map/while/body/eval_jaxpr/all_to_all | solution.py:68
  130.8 1.3 copy-start.1
  171.6 5.3 %copy-start = (f32[2,1,32,128,64]{4,3,2,0,1:T(8,128)S(1)}, f32[2,1,32,128,64]{4,3,2,0,1:T(8,128)}, u32[]{:S(2)}) copy-start(f32[2,1,32,128,64]{4,3,2,0,1:T(8,128)} %copy.90) | copy-start | bytes 6291460 | tf_op jit(solution)/shard_map/while
  252.9 29.6 %all-to-all-start = ((f32[2,1,128,2048]{3,0,1,2:T(2,128)}), f32[2,1,128,2048]{3,0,1,2:T(2,128)S(1)}, u32[]{:S(2)}, u32[]{:S(2)}) async-start(f32[2,1,128,2048]{3,0,1,2:T(2,128)} %convert_multiply_fusion.3), calls=%async_computation | async-start | bytes 4194304 | tf_op jit(solution)/shard_map/while/body/eval_jaxpr/all_to_all | solution.py:65
  288.0 2.0 copy-start.3
  288.0 2.0 copy-start.4
  309.5 35.9 %all-to-all-start.1 = ((f32[128,1,4096]{2,1,0:T(1,128)}), f32[128,1,4096]{2,1,0:T(1,128)S(1)}, u32[]{:S(2)}, u32[]{:S(2)}) async-start(f32[128,1,4096]{2,1,0:T(1,128)} %reshape.469), calls=%async_computation.1 | async-start | bytes 4194304 | tf_op jit(solution)/shard_map/while/body/eval_jaxpr/all_to_all | solution.py:68
  345.3 1.3 copy-start.1
  386.1 5.3 %copy-start = (f32[2,1,32,128,64]{4,3,2,0,1:T(8,128)S(1)}, f32[2,1,32,128,64]{4,3,2,0,1:T(8,128)}, u32[]{:S(2)}) copy-start(f32[2,1,32,128,64]{4,3,2,0,1:T(8,128)} %copy.90) | copy-start | bytes 6291460 | tf_op jit(solution)/shard_map/while
where the time goes:
time: 473 us; the launch traced here: 465 us
  local copies, waits for them, and re-layouts  231 us (49%)
  waiting for transfers between devices  106 us (22%)
  other arithmetic  42.6 us (9%)
  matrix products  33.6 us (7%)
  starting transfers between devices  26.3 us (6%)
  loops' own time  24.1 us (5%)
    rev x2, local copies, waits for them, and re-layouts, one_block(): jnp.flip(full_rows[:, :, 1:], 2)  67.1 us
    all_to_all x2, waiting for transfers between devices, one_block(): lax.all_to_all(columns, ('rows', 'cols'), split_axis=3, concat_axis=2, ti...  60 us
    all_to_all x6, local copies, waits for them, and re-layouts, one_block(): lax.all_to_all(columns, ('rows', 'cols'), split_axis=3, concat_axis=2, ti...  47.5 us
    all_to_all x2, waiting for transfers between devices, one_block(): lax.all_to_all(spectrum, 'cols', split_axis=2, concat_axis=3, tiled=True)  46.3 us
    while x20, local copies, waits for them, and re-layouts  41.2 us
    dot_general x8, matrix products, contract(): jnp.einsum(form, left, table, precision=lax.Precision.HIGHEST, preferred_...  33.6 us
    another operation x1, loops' own time, shards(): return lax.map(per_plane, (jnp.swapaxes(noise, 0, 1), root_eigen))  24.1 us
    div x4, local copies, waits for them, and re-layouts, along_rows(): return final.reshape(dims_of[1], dims_of[3], 2 * half_len) / scale_by  18.8 us
  transfers between devices with their start and end apart: 4, of which 4 were waited for; matrix products, arithmetic and copies ran while one was open for 1% of the time, Pallas kernels for 0%

commit v1 on v0

v1 whole, which is shorter than its diff:
```python
import numpy as np
import jax
import jax.numpy as jnp
from jax import lax
from jax.experimental import pallas as pl
from jax.experimental.pallas import tpu as pltpu
from jax.sharding import PartitionSpec as P

VMEM_LIMIT = 48 * 1024 * 1024


def split_bf16(table):
    hi = jnp.asarray(table, jnp.float32).astype(jnp.bfloat16)
    lo = (jnp.asarray(table, jnp.float32) - hi.astype(jnp.float32)).astype(jnp.bfloat16)
    return hi, lo


def unit(num, den):
    ang = 2.0 * np.pi * (np.asarray(num) % den) / den
    return np.cos(ang), np.sin(ang)


def lane_tables():
    step = np.arange(128)
    cos, sin = unit(step[:, None] * step[None, :], 128)
    matrix = np.block([[cos, -sin], [sin, cos]])
    cos, sin = unit(np.arange(64)[:, None] * step[None, :], 8192)
    twist = np.stack([cos, sin], 1).reshape(128, 128)
    return matrix, twist.astype(np.float32)


def row_tables():
    src = np.arange(128)
    blocks = []
    for parity in (0, 1):
        cos, sin = unit(src[:, None] * (2 * np.arange(128) + parity)[None, :], 256)
        blocks.append(np.block([[cos, sin], [-sin, cos]]))
    matrix = np.concatenate(blocks, 1) / 4096.0
    twist = np.zeros((32, 8, 128))
    for parity in (0, 1):
        cos, sin = unit(np.arange(32)[:, None] * (2 * np.arange(128) + parity)[None, :], 8192)
        twist[:, 2 * parity] = cos
        twist[:, 2 * parity + 1] = sin
    return matrix, twist.astype(np.float32)


def cadd(a, b):
    return a[0] + b[0], a[1] + b[1]


def csub(a, b):
    return a[0] - b[0], a[1] - b[1]


def turn(a):
    return -a[1], a[0]


def cmul(a, cos, sin):
    return a[0] * cos - a[1] * sin, a[0] * sin + a[1] * cos


def dft4(v):
    s, d = cadd(v[0], v[2]), csub(v[0], v[2])
    t, u = cadd(v[1], v[3]), turn(csub(v[1], v[3]))
    return [cadd(s, t), cadd(d, u), csub(s, t), csub(d, u)]


HALF = float(np.sqrt(0.5))


def dft8(v):
    even, odd = dft4(v[0::2]), dft4(v[1::2])
    one = odd[1]
    one = ((one[0] - one[1]) * HALF, (one[0] + one[1]) * HALF)
    three = odd[3]
    three = ((-three[0] - three[1]) * HALF, (three[0] - three[1]) * HALF)
    odd = [odd[0], one, turn(odd[2]), three]
    return [cadd(even[i], odd[i]) for i in range(4)] + [csub(even[i], odd[i]) for i in range(4)]


def dft8_real(v):
    even, odd = dft4(v[0::2]), dft4(v[1::2])
    one, three = odd[1], odd[3]
    odd_re = [odd[0][0], (one[0] - one[1]) * HALF, -odd[2][1], (-three[0] - three[1]) * HALF]
    return [even[i][0] + odd_re[i] for i in range(4)] + [even[i][0] - odd_re[i] for i in range(4)]


def const_mul(a, num, den):
    num %= den
    if num == 0:
        return a
    if num * 4 == den:
        return turn(a)
    cos, sin = unit(num, den)
    return cmul(a, float(cos), float(sin))


def parts(x):
    hi = x.astype(jnp.bfloat16)
    return hi, (x - hi.astype(jnp.float32)).astype(jnp.bfloat16)


def spectrum_kernel(noise_ref, root_ref, out_ref):
    root = root_ref[0].astype(jnp.float32)
    out_ref[0, 0] = noise_ref[0, 0].astype(jnp.float32) * root
    out_ref[0, 1] = noise_ref[1, 0].astype(jnp.float32) * root


def spectrum(noise, root, plane):
    return pl.pallas_call(
        spectrum_kernel,
        grid=(4,),
        in_specs=[
            pl.BlockSpec((2, 1, 32, 2048), lambda i: (0, plane, i, 0)),
            pl.BlockSpec((1, 32, 2048), lambda i: (plane, i, 0)),
        ],
        out_specs=pl.BlockSpec((1, 2, 32, 2048), lambda i: (i, 0, 0, 0)),
        out_shape=jax.ShapeDtypeStruct((4, 2, 32, 2048), jnp.float32),
        compiler_params=pltpu.CompilerParams(vmem_limit_bytes=VMEM_LIMIT),
        cost_estimate=pl.CostEstimate(flops=1 << 20, bytes_accessed=7 << 19, transcendentals=0),
        name="spectrum",
    )(noise, root)


def columns_kernel(x_ref, hi_ref, lo_ref, twist_ref, out_ref, mid, turned):
    for low in range(8):
        v = []
        for high in range(8):
            block, col = high // 2, (high % 2) * 8 + low
            v.append(tuple(x_ref[block, s, :, col * 128:(col + 1) * 128] for s in (0, 1)))
        for b, value in enumerate(dft8(v)):
            value = const_mul(value, low * b, 64)
            for s in (0, 1):
                mid[s, b, low] = value[s]
    for b in range(8):
        v = [(mid[0, b, low], mid[1, b, low]) for low in range(8)]
        for h, value in enumerate(dft8(v)):
            y_low = b + 8 * h
            value = cmul(value, twist_ref[2 * y_low:2 * y_low + 1, :], twist_ref[2 * y_low + 1:2 * y_low + 2, :])
            for s in (0, 1):
                turned[s, pl.ds(y_low, 8, stride=64), :] = value[s]
    flat = out_ref.reshape(128 * 8, 128)
    dims = (((1,), (1,)), ((), ()))
    for half in range(2):
        rows = slice(half * 256, half * 256 + 256)
        hi, lo = parts(jnp.concatenate([turned[0, rows, :], turned[1, rows, :]], 1))
        result = lax.dot_general(hi_ref[...], hi, dims, preferred_element_type=jnp.float32)
        result += lax.dot_general(lo_ref[...], hi, dims, preferred_element_type=jnp.float32)
        result += lax.dot_general(hi_ref[...], lo, dims, preferred_element_type=jnp.float32)
        for pair in range(2):
            for s in (0, 1):
                flat[pl.ds((half * 2 + pair) * 2 + s, 128, stride=8), :] = result[
                    s * 128:(s + 1) * 128, pair * 128:(pair + 1) * 128
                ]


def columns(whole, hi, lo, twist):
    return pl.pallas_call(
        columns_kernel,
        grid=(4,),
        in_specs=[
            pl.BlockSpec((4, 2, 8, 2048), lambda i: (0, 0, i, 0)),
            pl.BlockSpec((256, 256), lambda i: (0, 0)),
            pl.BlockSpec((256, 256), lambda i: (0, 0)),
            pl.BlockSpec((128, 128), lambda i: (0, 0)),
        ],
        out_specs=pl.BlockSpec((128, 8, 128), lambda i: (0, i, 0)),
        out_shape=jax.ShapeDtypeStruct((128, 32, 128), jnp.float32),
        scratch_shapes=[
            pltpu.VMEM((2, 8, 8, 8, 128), jnp.float32),
            pltpu.VMEM((2, 512, 128), jnp.float32),
        ],
        compiler_params=pltpu.CompilerParams(vmem_limit_bytes=VMEM_LIMIT),
        cost_estimate=pl.CostEstimate(flops=3 << 28, bytes_accessed=4 << 20, transcendentals=0),
        name="columns",
    )(whole, hi, lo, twist)


def rows_kernel(c_ref, hi_ref, lo_ref, twist_ref, *rest):
    out_ref, steps = rest[-2:]
    flat = c_ref.reshape(128 * 32, 128)

    def one_pair(pair, _):
        re = flat[pl.ds(2 * pair, 128, stride=32), :]
        im = flat[pl.ds(2 * pair + 1, 128, stride=32), :]
        both = jnp.concatenate([re.T, im.T], 1)
        hi, lo = parts(both)
        result = jnp.dot(hi, hi_ref[...], preferred_element_type=jnp.float32)
        result += jnp.dot(hi, lo_ref[...], preferred_element_type=jnp.float32)
        result += jnp.dot(lo, hi_ref[...], preferred_element_type=jnp.float32)
        for k in (0, 1):
            rows = slice(64 * k, 64 * k + 64)
            for parity in (0, 1):
                at = parity * 256
                value = (result[rows, at:at + 128], result[rows, at + 128:at + 256])
                value = cmul(
                    value,
                    twist_ref[2 * pair + k, 2 * parity:2 * parity + 1, :],
                    twist_ref[2 * pair + k, 2 * parity + 1:2 * parity + 2, :],
                )
                for s in (0, 1):
                    steps[2 * parity + s, 2 * pair + k] = value[s]
        @pl.when(pair == 0)
        def _():
            steps[0, 0] -= im.T[0:64, 0:1] * (1.0 / 4096.0)
            steps[2, 0] -= re.T[0:64, 0:1] * (1.0 / 4096.0)
        return 0

    lax.fori_loop(0, 16, one_pair, 0)

    def one_group(group, _):
        at = pl.multiple_of(group * 8, 8)
        for parity in (0, 1):
            mid = [[None] * 8 for _ in range(4)]
            for low in range(8):
                v = [tuple(steps[2 * parity + s, 8 * high + low, pl.ds(at, 8), :] for s in (0, 1)) for high in range(4)]
                for b, value in enumerate(dft4(v)):
                    mid[b][low] = const_mul(value, low * b, 32)
            for b in range(4):
                for h, value in enumerate(dft8_real(mid[b])):
                    col = (parity * 32 + b + 4 * h) * 128
                    out_ref[0, pl.ds(at, 8), col:col + 128] = value
        return 0

    lax.fori_loop(0, 8, one_group, 0)


def rows(full, hi, lo, twist, plane, field=None):
    whole = lambda *dims: pl.BlockSpec(dims, lambda i: (0,) * len(dims))
    operands = [full, hi, lo, twist]
    specs = [whole(128, 32, 128), whole(256, 512), whole(256, 512), whole(32, 8, 128)]
    if field is not None:
        operands.append(field)
        specs.append(pl.BlockSpec(memory_space=pl.ANY))
    return pl.pallas_call(
        rows_kernel,
        grid=(1,),
        in_specs=specs,
        out_specs=pl.BlockSpec((1, 64, 8192), lambda i: (plane, 0, 0)),
        out_shape=jax.ShapeDtypeStruct((2, 64, 8192), jnp.float32),
        scratch_shapes=[pltpu.VMEM((4, 32, 64, 128), jnp.float32)],
        input_output_aliases={} if field is None else {4: 0},
        compiler_params=pltpu.CompilerParams(vmem_limit_bytes=VMEM_LIMIT),
        cost_estimate=pl.CostEstimate(flops=3 << 29, bytes_accessed=4 << 20, transcendentals=0),
        name="rows",
    )(*operands)


def shards(noise, root):
    lane_matrix, lane_twist = lane_tables()
    row_matrix, row_twist = row_tables()
    lane_hi, lane_lo = split_bf16(lane_matrix)
    row_hi, row_lo = split_bf16(row_matrix)
    field = None
    full = []
    for plane in range(2):
        sent = spectrum(noise, root, plane)
        whole = lax.all_to_all(sent, "cols", 0, 0, tiled=True)
        blocks = columns(whole, lane_hi, lane_lo, jnp.asarray(lane_twist))
        full.append(lax.all_to_all(blocks, ("rows", "cols"), 0, 0, tiled=True))
    for plane in range(2):
        field = rows(full[plane], row_hi, row_lo, jnp.asarray(row_twist), plane, field)
    return field


def solution(mesh):
    return jax.shard_map(
        shards,
        mesh=mesh,
        in_specs=(P(None, None, "rows", "cols"), P(None, "rows", "cols")),
        out_specs=P(None, ("rows", "cols"), None),
        check_vma=False,
    )
```

time: 473 us -> 151 us (0.32); the launches traced: 465 us -> 151 us
  local copies, waits for them, and re-layouts: 231 us -> 8.1 us
  other arithmetic: 42.6 us -> 0 us
  matrix products: 33.6 us -> 0 us
  Pallas kernels: 0 us -> 28.5 us
  loops' own time: 24.1 us -> 0 us
  waiting for transfers between devices: 106 us -> 86 us
    rev x2 -> x0, local copies, waits for them, and re-layouts: 67.1 us -> none  [one_block(): jnp.flip(full_rows[:, :, 1:], 2)]
    all_to_all x8 -> x0, local copies, waits for them, and re-layouts: 53.7 us -> none  [the longest x6 47.5 us: one_block(): lax.all_to_all(columns, ('rows', 'cols'), split_axis=3, concat_axis=2, ti...]
    while x20 -> x0, local copies, waits for them, and re-layouts: 41.2 us -> none
    dot_general x8 -> x0, matrix products: 33.6 us -> none  [contract(): jnp.einsum(form, left, table, precision=lax.Precision.HIGHEST, preferred_...]
    pallas_call x0 -> x6, Pallas kernels: none -> 28.5 us  [the longest x2 18.2 us: rows(): pl.pallas_call(rows_kernel, grid=(1,), in_specs=specs, out_specs=pl.Block...]
    another operation x1 -> x0, loops' own time: 24.1 us -> none  [shards(): return lax.map(per_plane, (jnp.swapaxes(noise, 0, 1), root_eigen))]
    all_to_all x4, waiting for transfers between devices: 106 us -> 86 us  [the longest x2 44.5 us: shards(): full.append(lax.all_to_all(blocks, ('rows', 'cols'), 0, 0, tiled=True))]
    slice x10 -> x0, local copies, waits for them, and re-layouts: 19.2 us -> none  [the longest x2 9.13 us: one_block(): full_rows[:, :, 1:]]
  transfers between devices with their start and end apart: 4 -> 4, of which waited for: 4 -> 4; matrix products, arithmetic and copies ran while one was open for 1% -> 0% of each run, Pallas kernels for 0% -> 13%
where the time goes in v1:
time: 151 us
  waiting for transfers between devices  86 us (57%)
  Pallas kernels  28.5 us (19%)
  starting transfers between devices  27.9 us (18%)
  local copies, waits for them, and re-layouts  8.1 us (5%)
    all_to_all x2, waiting for transfers between devices, shards(): full.append(lax.all_to_all(blocks, ('rows', 'cols'), 0, 0, tiled=True))  44.5 us
    all_to_all x2, waiting for transfers between devices, shards(): whole = lax.all_to_all(sent, 'cols', 0, 0, tiled=True)  41.5 us
    pallas_call x2, Pallas kernels, rows(): pl.pallas_call(rows_kernel, grid=(1,), in_specs=specs, out_specs=pl.Block...  18.2 us
    all_to_all x2, starting transfers between devices, shards(): full.append(lax.all_to_all(blocks, ('rows', 'cols'), 0, 0, tiled=True))  17.4 us
    all_to_all x2, starting transfers between devices, shards(): whole = lax.all_to_all(sent, 'cols', 0, 0, tiled=True)  10.5 us
    pallas_call x2, Pallas kernels, columns(): pl.pallas_call(columns_kernel, grid=(4,), in_specs=[pl.BlockSpec((4, 2, 8...  9.53 us
    unnamed x28, local copies, waits for them, and re-layouts  8.1 us
  transfers between devices with their start and end apart: 4, of which 4 were waited for; matrix products, arithmetic and copies ran while one was open for 0% of the time, Pallas kernels for 13%

profile of v1, /device:TPU:1, one launch (start us, length us, event | category | flops | bytes accessed | tf_op | source)
XLA Modules:
  0.0 150.6 jit_solution(5512473339081851133)
XLA Ops:
  0.0 1.6 %copy-done = bf16[2,2,128,2048]{3,2,1,0:T(8,128)(2,1)S(1)} copy-done((bf16[2,2,128,2048]{3,2,1,0:T(8,128)(2,1)S(1)}, bf16[2,2,128,2048]{3,2,1,0:T(8,128)(2,1)}, u32[]{:S(2)}) %copy-start) | copy-done | bytes 2097176
  1.6 1.2 copy-done.6
  2.8 0.4 spectrum.3
  3.2 0.0 copy-start.5
  3.2 1.3 copy-done.5
  4.5 6.1 %all-to-all-start.2 = ((f32[4,2,32,2048]{3,2,1,0:T(8,128)}), f32[4,2,32,2048]{3,2,1,0:T(8,128)}, u32[]{:S(2)}, u32[]{:S(2)}) async-start(f32[4,2,32,2048]{3,2,1,0:T(8,128)} %copy-done.5), calls=%async_computation.2 | async-start | bytes 4194304 | tf_op jit(solution)/shard_map/all_to_all | solution.py:259
  10.6 0.0 copy-done.1
  10.6 0.0 copy-done.7
  10.6 0.4 spectrum.2
  11.0 0.0 copy-start.4
  11.0 1.3 copy-done.4
  12.3 23.2 %all-to-all-done.2.x_ref = f32[4,2,32,2048]{3,2,1,0:T(8,128)} async-done(((f32[4,2,32,2048]{3,2,1,0:T(8,128)}), f32[4,2,32,2048]{3,2,1,0:T(8,128)}, u32[]{:S(2)}, u32[]{:S(2)}) %all-to-all-start.2) | async-done | bytes 2097184 | tf_op jit(solution)/shard_map/all_to_all | solution.py:259
  35.5 4.4 %all-to-all-start = ((f32[4,2,32,2048]{3,2,1,0:T(8,128)}), f32[4,2,32,2048]{3,2,1,0:T(8,128)S(1)}, u32[]{:S(2)}, u32[]{:S(2)}) async-start(f32[4,2,32,2048]{3,2,1,0:T(8,128)} %copy-done.4), calls=%async_computation | async-start | bytes 4194304 | tf_op jit(solution)/shard_map/all_to_all | solution.py:259
  40.0 0.0 copy-done.11
  40.0 0.0 copy-done.12
  40.0 0.0 copy-done.13
  40.0 5.2 %columns.3 = f32[128,32,128]{2,1,0:T(8,128)S(1)} custom-call(f32[4,2,32,2048]{3,2,1,0:T(8,128)} %all-to-all-done.2.x_ref, bf16[256,256]{1,0:T(8,128)(2,1)S(1)} %copy-done.12, bf16[256,256]{1,0:T(8,128)(2,1)S(1)} %copy-done.11, f32[128,128]{1,0:T(8,128)S(1)} %copy-done.13), custom_call_target="tpu_custom_call" | custom-call | flops 805306368 | bytes 4194304 | tf_op jit(solution)/shard_map/columns/pallas_call | solution.py:159
  45.2 0.0 copy-start.2
  45.2 1.3 copy-done.2
  46.6 18.3 %all-to-all-done.x_ref = f32[4,2,32,2048]{3,2,1,0:T(8,128)S(1)} async-done(((f32[4,2,32,2048]{3,2,1,0:T(8,128)}), f32[4,2,32,2048]{3,2,1,0:T(8,128)S(1)}, u32[]{:S(2)}, u32[]{:S(2)}) %all-to-all-start) | async-done | bytes 2097184 | tf_op jit(solution)/shard_map/all_to_all | solution.py:259
  64.8 11.4 %all-to-all-start.3 = ((f32[128,32,128]{2,1,0:T(8,128)}), f32[128,32,128]{2,1,0:T(8,128)}, u32[]{:S(2)}, u32[]{:S(2)}) async-start(f32[128,32,128]{2,1,0:T(8,128)} %copy-done.2), calls=%async_computation.3 | async-start | bytes 4194304 | tf_op jit(solution)/shard_map/all_to_all | solution.py:261
  76.2 4.3 %columns.2 = f32[128,32,128]{2,1,0:T(8,128)S(1)} custom-call(f32[4,2,32,2048]{3,2,1,0:T(8,128)S(1)} %all-to-all-done.x_ref, bf16[256,256]{1,0:T(8,128)(2,1)S(1)} %copy-done.12, bf16[256,256]{1,0:T(8,128)(2,1)S(1)} %copy-done.11, f32[128,128]{1,0:T(8,128)S(1)} %copy-done.13), custom_call_target="tpu_custom_call" | custom-call | flops 805306368 | bytes 4194304 | tf_op jit(solution)/shard_map/columns/pallas_call | solution.py:159
  80.6 0.0 copy-start.3
  80.6 1.3 copy-done.3
  81.9 24.2 %all-to-all-done.3.c_ref = f32[128,32,128]{2,1,0:T(8,128)} async-done(((f32[128,32,128]{2,1,0:T(8,128)}), f32[128,32,128]{2,1,0:T(8,128)}, u32[]{:S(2)}, u32[]{:S(2)}) %all-to-all-start.3) | async-done | bytes 2097184 | tf_op jit(solution)/shard_map/all_to_all | solution.py:261
  106.1 5.9 %all-to-all-start.1 = ((f32[128,32,128]{2,1,0:T(8,128)}), f32[128,32,128]{2,1,0:T(8,128)S(1)}, u32[]{:S(2)}, u32[]{:S(2)}) async-start(f32[128,32,128]{2,1,0:T(8,128)} %copy-done.3), calls=%async_computation.1 | async-start | bytes 4194304 | tf_op jit(solution)/shard_map/all_to_all | solution.py:261
  112.1 0.0 copy-done.8
  112.1 0.0 copy-done.9
  112.1 0.0 copy-done.10
  112.1 9.9 %rows.2.rest_0_ = f32[2,64,8192]{2,1,0:T(8,128)} custom-call(f32[128,32,128]{2,1,0:T(8,128)} %all-to-all-done.3.c_ref, bf16[256,512]{1,0:T(8,128)(2,1)S(1)} %copy-done.9, bf16[256,512]{1,0:T(8,128)(2,1)S(1)} %copy-done.8, f32[32,8,128]{2,1,0:T(8,128)S(1)} %copy-done.10), custom_call_target="tpu_custom_call" | custom-call | flops 1610612736 | bytes 4194304 | tf_op jit(solution)/shard_map/rows/pallas_call | solution.py:236
  122.0 20.3 %all-to-all-done.1.c_ref = f32[128,32,128]{2,1,0:T(8,128)S(1)} async-done(((f32[128,32,128]{2,1,0:T(8,128)}), f32[128,32,128]{2,1,0:T(8,128)S(1)}, u32[]{:S(2)}, u32[]{:S(2)}) %all-to-all-start.1) | async-done | bytes 2097184 | tf_op jit(solution)/shard_map/all_to_all | solution.py:261
  142.3 8.3 %rows.3 = f32[2,64,8192]{2,1,0:T(8,128)} custom-call(f32[128,32,128]{2,1,0:T(8,128)S(1)} %all-to-all-done.1.c_ref, bf16[256,512]{1,0:T(8,128)(2,1)S(1)} %copy-done.9, bf16[256,512]{1,0:T(8,128)(2,1)S(1)} %copy-done.8, f32[32,8,128]{2,1,0:T(8,128)S(1)} %copy-done.10, f32[2,64,8192]{2,1,0:T(8,128)} %rows.2.rest_0_), custom_call_target="tpu_custom_call", output_to_operand_aliasing={{}: (4, {})} | custom-call | flops 1610612736 | bytes 4194304 | tf_op jit(solution)/shard_map/rows/pallas_call | solution.py:236
  (10 shorter events, 0.0 us)
Async XLA Ops:
  0.0 1.6 %copy-start = (bf16[2,2,128,2048]{3,2,1,0:T(8,128)(2,1)S(1)}, bf16[2,2,128,2048]{3,2,1,0:T(8,128)(2,1)}, u32[]{:S(2)}) copy-start(bf16[2,2,128,2048]{3,2,1,0:T(8,128)(2,1)} %noise_ref.3) | copy-start | bytes 6291460
  1.6 1.2 copy-start.6
  3.2 1.3 copy-start.5
  4.5 6.1 %copy-start.1 = (bf16[2,2,128,2048]{3,2,1,0:T(8,128)(2,1)S(1)}, bf16[2,2,128,2048]{3,2,1,0:T(8,128)(2,1)}, u32[]{:S(2)}) copy-start(bf16[2,2,128,2048]{3,2,1,0:T(8,128)(2,1)} %noise_ref.3) | copy-start | bytes 6291460
  4.5 6.1 %copy-start.7 = (bf16[2,128,2048]{2,1,0:T(8,128)(2,1)S(1)}, bf16[2,128,2048]{2,1,0:T(8,128)(2,1)}, u32[]{:S(2)}) copy-start(bf16[2,128,2048]{2,1,0:T(8,128)(2,1)} %root_ref.3) | copy-start | bytes 3145732
  4.5 31.0 %all-to-all-start.2 = ((f32[4,2,32,2048]{3,2,1,0:T(8,128)}), f32[4,2,32,2048]{3,2,1,0:T(8,128)}, u32[]{:S(2)}, u32[]{:S(2)}) async-start(f32[4,2,32,2048]{3,2,1,0:T(8,128)} %copy-done.5), calls=%async_computation.2 | async-start | bytes 4194304 | tf_op jit(solution)/shard_map/all_to_all | solution.py:259
  11.0 1.3 copy-start.4
  12.3 27.7 %copy-start.11 = (bf16[256,256]{1,0:T(8,128)(2,1)S(1)}, bf16[256,256]{1,0:T(8,128)(2,1)}, u32[]{:S(2)}) copy-start(bf16[256,256]{1,0:T(8,128)(2,1)} %constant.15.lo_ref) | copy-start | bytes 393220
  12.3 27.7 %copy-start.12 = (bf16[256,256]{1,0:T(8,128)(2,1)S(1)}, bf16[256,256]{1,0:T(8,128)(2,1)}, u32[]{:S(2)}) copy-start(bf16[256,256]{1,0:T(8,128)(2,1)} %constant.12.hi_ref) | copy-start | bytes 393220
  12.3 27.7 %copy-start.13 = (f32[128,128]{1,0:T(8,128)S(1)}, f32[128,128]{1,0:T(8,128)}, u32[]{:S(2)}) copy-start(f32[128,128]{1,0:T(8,128)} %constant.10.clone.twist_ref) | copy-start | bytes 196612
  35.5 29.3 %all-to-all-start = ((f32[4,2,32,2048]{3,2,1,0:T(8,128)}), f32[4,2,32,2048]{3,2,1,0:T(8,128)S(1)}, u32[]{:S(2)}, u32[]{:S(2)}) async-start(f32[4,2,32,2048]{3,2,1,0:T(8,128)} %copy-done.4), calls=%async_computation | async-start | bytes 4194304 | tf_op jit(solution)/shard_map/all_to_all | solution.py:259
  45.2 1.3 copy-start.2
  64.8 41.3 %all-to-all-start.3 = ((f32[128,32,128]{2,1,0:T(8,128)}), f32[128,32,128]{2,1,0:T(8,128)}, u32[]{:S(2)}, u32[]{:S(2)}) async-start(f32[128,32,128]{2,1,0:T(8,128)} %copy-done.2), calls=%async_computation.3 | async-start | bytes 4194304 | tf_op jit(solution)/shard_map/all_to_all | solution.py:261
  80.6 1.3 copy-start.3
  81.9 30.2 %copy-start.8 = (bf16[256,512]{1,0:T(8,128)(2,1)S(1)}, bf16[256,512]{1,0:T(8,128)(2,1)}, u32[]{:S(2)}) copy-start(bf16[256,512]{1,0:T(8,128)(2,1)} %constant.19.lo_ref) | copy-start | bytes 786436
  81.9 30.2 %copy-start.9 = (bf16[256,512]{1,0:T(8,128)(2,1)S(1)}, bf16[256,512]{1,0:T(8,128)(2,1)}, u32[]{:S(2)}) copy-start(bf16[256,512]{1,0:T(8,128)(2,1)} %constant.16.hi_ref) | copy-start | bytes 786436
  81.9 30.2 %copy-start.10 = (f32[32,8,128]{2,1,0:T(8,128)S(1)}, f32[32,8,128]{2,1,0:T(8,128)}, u32[]{:S(2)}) copy-start(f32[32,8,128]{2,1,0:T(8,128)} %constant.11.clone.twist_ref) | copy-start | bytes 393220
  106.1 36.2 %all-to-all-start.1 = ((f32[128,32,128]{2,1,0:T(8,128)}), f32[128,32,128]{2,1,0:T(8,128)S(1)}, u32[]{:S(2)}, u32[]{:S(2)}) async-start(f32[128,32,128]{2,1,0:T(8,128)} %copy-done.3), calls=%async_computation.1 | async-start | bytes 4194304 | tf_op jit(solution)/shard_map/all_to_all | solution.py:261

commit v2 on v1

--- a/solution.py
+++ b/solution.py
@@ -101,34 +101,48 @@
     return hi, (x - hi.astype(jnp.float32)).astype(jnp.bfloat16)
 
 
-def spectrum_kernel(noise_ref, root_ref, out_ref):
-    root = root_ref[0].astype(jnp.float32)
-    out_ref[0, 0] = noise_ref[0, 0].astype(jnp.float32) * root
-    out_ref[0, 1] = noise_ref[1, 0].astype(jnp.float32) * root
-
-
-def spectrum(noise, root, plane):
+def spectrum_kernel(col_ref, noise_ref, root_ref, *outs):
+    for plane in range(2):
+        for d in range(4):
+            rows = pl.ds(pl.multiple_of((col_ref[0] ^ d) * 32, 32), 32)
+            root = root_ref[plane, rows, :].astype(jnp.float32)
+            for s in (0, 1):
+                outs[4 * plane + d][s] = noise_ref[s, plane, rows, :].astype(jnp.float32) * root
+
+
+def spectrum(col, noise, root):
     return pl.pallas_call(
         spectrum_kernel,
-        grid=(4,),
-        in_specs=[
-            pl.BlockSpec((2, 1, 32, 2048), lambda i: (0, plane, i, 0)),
-            pl.BlockSpec((1, 32, 2048), lambda i: (plane, i, 0)),
-        ],
-        out_specs=pl.BlockSpec((1, 2, 32, 2048), lambda i: (i, 0, 0, 0)),
-        out_shape=jax.ShapeDtypeStruct((4, 2, 32, 2048), jnp.float32),
+        grid_spec=pltpu.PrefetchScalarGridSpec(
+            num_scalar_prefetch=1,
+            grid=(1,),
+            in_specs=[
+                pl.BlockSpec((2, 2, 128, 2048), lambda i, c: (0, 0, 0, 0)),
+                pl.BlockSpec((2, 128, 2048), lambda i, c: (0, 0, 0)),
+            ],
+            out_specs=[pl.BlockSpec((2, 32, 2048), lambda i, c: (0, 0, 0))] * 8,
+        ),
+        out_shape=[jax.ShapeDtypeStruct((2, 32, 2048), jnp.float32)] * 8,
         compiler_params=pltpu.CompilerParams(vmem_limit_bytes=VMEM_LIMIT),
-        cost_estimate=pl.CostEstimate(flops=1 << 20, bytes_accessed=7 << 19, transcendentals=0),
+        cost_estimate=pl.CostEstimate(flops=1 << 21, bytes_accessed=7 << 20, transcendentals=0),
         name="spectrum",
-    )(noise, root)
-
-
-def columns_kernel(x_ref, hi_ref, lo_ref, twist_ref, out_ref, mid, turned):
+    )(col, noise, root)
+
+
+def by_index(values, index):
+    odd, upper = (index & 1) == 1, (index & 2) == 2
+    pick = lambda flag, a, b: tuple(jnp.where(flag, p, q) for p, q in zip(a, b))
+    v = [pick(odd, values[d ^ 1], values[d]) for d in range(4)]
+    return [pick(upper, v[d ^ 2], v[d]) for d in range(4)]
+
+
+def columns_kernel(col_ref, x0, x1, x2, x3, hi_ref, lo_ref, twist_ref, out_ref, mid, turned):
     for low in range(8):
-        v = []
-        for high in range(8):
-            block, col = high // 2, (high % 2) * 8 + low
-            v.append(tuple(x_ref[block, s, :, col * 128:(col + 1) * 128] for s in (0, 1)))
+        v = [None] * 8
+        for half in range(2):
+            at = (half * 8 + low) * 128
+            got = [tuple(x[s, :, at:at + 128] for s in (0, 1)) for x in (x0, x1, x2, x3)]
+            v[half::2] = by_index(got, col_ref[0])
         for b, value in enumerate(dft8(v)):
             value = const_mul(value, low * b, 64)
             for s in (0, 1):
@@ -155,26 +169,29 @@
                 ]
 
 
-def columns(whole, hi, lo, twist):
+def columns(col, pieces, hi, lo, twist, flops):
     return pl.pallas_call(
         columns_kernel,
-        grid=(4,),
-        in_specs=[
-            pl.BlockSpec((4, 2, 8, 2048), lambda i: (0, 0, i, 0)),
-            pl.BlockSpec((256, 256), lambda i: (0, 0)),
-            pl.BlockSpec((256, 256), lambda i: (0, 0)),
-            pl.BlockSpec((128, 128), lambda i: (0, 0)),
-        ],
-        out_specs=pl.BlockSpec((128, 8, 128), lambda i: (0, i, 0)),
+        grid_spec=pltpu.PrefetchScalarGridSpec(
+            num_scalar_prefetch=1,
+            grid=(4,),
+            in_specs=[pl.BlockSpec((2, 8, 2048), lambda i, c: (0, i, 0))] * 4
+            + [
+                pl.BlockSpec((256, 256), lambda i, c: (0, 0)),
+                pl.BlockSpec((256, 256), lambda i, c: (0, 0)),
+                pl.BlockSpec((128, 128), lambda i, c: (0, 0)),
+            ],
+            out_specs=pl.BlockSpec((128, 8, 128), lambda i, c: (0, i, 0)),
+            scratch_shapes=[
+                pltpu.VMEM((2, 8, 8, 8, 128), jnp.float32),
+                pltpu.VMEM((2, 512, 128), jnp.float32),
+            ],
+        ),
         out_shape=jax.ShapeDtypeStruct((128, 32, 128), jnp.float32),
-        scratch_shapes=[
-            pltpu.VMEM((2, 8, 8, 8, 128), jnp.float32),
-            pltpu.VMEM((2, 512, 128), jnp.float32),
-        ],
         compiler_params=pltpu.CompilerParams(vmem_limit_bytes=VMEM_LIMIT),
-        cost_estimate=pl.CostEstimate(flops=3 << 28, bytes_accessed=4 << 20, transcendentals=0),
+        cost_estimate=pl.CostEstimate(flops=flops, bytes_accessed=4 << 20, transcendentals=0),
         name="columns",
-    )(whole, hi, lo, twist)
+    )(col, *pieces, hi, lo, twist)
 
 
 def rows_kernel(c_ref, hi_ref, lo_ref, twist_ref, *rest):
@@ -252,12 +269,18 @@
     row_matrix, row_twist = row_tables()
     lane_hi, lane_lo = split_bf16(lane_matrix)
     row_hi, row_lo = split_bf16(row_matrix)
+    col = lax.axis_index("cols")[None]
     field = None
     full = []
-    for plane in range(2):
-        sent = spectrum(noise, root, plane)
-        whole = lax.all_to_all(sent, "cols", 0, 0, tiled=True)
-        blocks = columns(whole, lane_hi, lane_lo, jnp.asarray(lane_twist))
+    sent = spectrum(col, noise, root)
+    got = [sent[0:4], sent[4:8]]
+    for plane in range(2):
+        got[plane] = list(got[plane])
+        for d in (2, 3, 1):
+            got[plane][d] = lax.ppermute(got[plane][d], "cols", [(c, c ^ d) for c in range(4)])
+    for plane in range(2):
+        pieces = got[plane]
+        blocks = columns(col, pieces, lane_hi, lane_lo, jnp.asarray(lane_twist), 3 << (28 + 8 * plane))
         full.append(lax.all_to_all(blocks, ("rows", "cols"), 0, 0, tiled=True))
     for plane in range(2):
         field = rows(full[plane], row_hi, row_lo, jnp.asarray(row_twist), plane, field)

time: 151 us -> 126 us (0.83)
  waiting for transfers between devices: 86 us -> 69.7 us
  starting transfers between devices: 27.9 us -> 22.3 us
  local copies, waits for them, and re-layouts: 8.1 us -> 2.56 us
  Pallas kernels: 28.5 us -> 30.5 us
    all_to_all x2 -> x0, waiting for transfers between devices: 41.5 us -> none  [shards(): whole = lax.all_to_all(sent, 'cols', 0, 0, tiled=True)]
    ppermute x0 -> x6, waiting for transfers between devices: none -> 40.6 us  [shards(): lax.ppermute(got[plane][d], 'cols', [(c, c ^ d) for c in range(4)])]
    all_to_all x2, waiting for transfers between devices: 44.5 us -> 29.1 us  [shards(): full.append(lax.all_to_all(blocks, ('rows', 'cols'), 0, 0, tiled=True))]
    all_to_all x2 -> x0, starting transfers between devices: 10.5 us -> none  [shards(): whole = lax.all_to_all(sent, 'cols', 0, 0, tiled=True)]
    unnamed x28 -> x16, local copies, waits for them, and re-layouts: 8.1 us -> 2.56 us
    ppermute x0 -> x6, starting transfers between devices: none -> 5.37 us  [shards(): lax.ppermute(got[plane][d], 'cols', [(c, c ^ d) for c in range(4)])]
    pallas_call x4 -> x3, Pallas kernels: 10.2 us -> 12.3 us  [the longest x2 10.3 us: columns(): pl.pallas_call(columns_kernel, grid_spec=pltpu.PrefetchScalarGridSpec(num...]
  transfers between devices with their start and end apart: 4 -> 8, of which waited for: 4 -> 5; matrix products, arithmetic and copies ran while one was open for 0% -> 0% of each run, Pallas kernels for 13% -> 16%
where the time goes in v2:
time: 126 us; the launch traced here: 125 us
  waiting for transfers between devices  69.7 us (55%)
  Pallas kernels  30.5 us (24%)
  starting transfers between devices  22.3 us (18%)
  local copies, waits for them, and re-layouts  2.56 us (2%)
    ppermute x6, waiting for transfers between devices, shards(): lax.ppermute(got[plane][d], 'cols', [(c, c ^ d) for c in range(4)])  40.6 us
    all_to_all x2, waiting for transfers between devices, shards(): full.append(lax.all_to_all(blocks, ('rows', 'cols'), 0, 0, tiled=True))  29.1 us
    pallas_call x2, Pallas kernels, rows(): pl.pallas_call(rows_kernel, grid=(1,), in_specs=specs, out_specs=pl.Block...  18.2 us
    all_to_all x2, starting transfers between devices, shards(): full.append(lax.all_to_all(blocks, ('rows', 'cols'), 0, 0, tiled=True))  16.9 us
    pallas_call x2, Pallas kernels, columns(): pl.pallas_call(columns_kernel, grid_spec=pltpu.PrefetchScalarGridSpec(num...  10.3 us
    ppermute x6, starting transfers between devices, shards(): lax.ppermute(got[plane][d], 'cols', [(c, c ^ d) for c in range(4)])  5.37 us
    unnamed x16, local copies, waits for them, and re-layouts  2.56 us
  transfers between devices with their start and end apart: 8, of which 5 were waited for; matrix products, arithmetic and copies ran while one was open for 0% of the time, Pallas kernels for 16%

profile of v2, /device:TPU:1, one launch (start us, length us, event | category | flops | bytes accessed | tf_op | source)
XLA Modules:
  0.0 125.2 jit_solution(18329281620838585697)
XLA Ops:
  0.0 0.0 copy-start.1
  0.0 1.2 copy-done.1
  1.2 0.0 copy-start.5
  1.2 2.0 %spectrum.1 = (f32[2,32,2048]{2,1,0:T(8,128)S(1)}, f32[2,32,2048]{2,1,0:T(8,128)S(1)}, f32[2,32,2048]{2,1,0:T(8,128)S(1)}, f32[2,32,2048]{2,1,0:T(8,128)S(1)}, f...) custom-call(s32[1]{0:T(128)} %bitcast.col_ref, ...), custom_call_target="tpu_custom_call" | custom-call | flops 2097152 | bytes 7340032 | tf_op jit(solution)/shard_map/spectrum/pallas_call | solution.py:114
  3.3 1.5 %collective-permute-start.3 = (f32[2,32,2048]{2,1,0:T(8,128)S(1)}, f32[2,32,2048]{2,1,0:T(8,128)S(1)}, u32[]{:S(2)}, u32[]{:S(2)}) collective-permute-start(f32[2,32,2048]{2,1,0:T(8,128)S(1)} %get-tuple-element.18), channel_id=1, source_target_pairs={{0,1},{1,0},{2,3},{3,2},{4,5},{5,4},{6,7},{7,6},{8,9},{9,8},{10,11... | collective-permute-start | bytes 1572872 | tf_op jit(solution)/shard_map/ppermute | solution.py:280
  4.8 1.4 %collective-permute-start.4 = (f32[2,32,2048]{2,1,0:T(8,128)S(1)}, f32[2,32,2048]{2,1,0:T(8,128)S(1)}, u32[]{:S(2)}, u32[]{:S(2)}) collective-permute-start(f32[2,32,2048]{2,1,0:T(8,128)S(1)} %get-tuple-element.19), channel_id=1, source_target_pairs={{0,2},{1,3},{2,0},{3,1},{4,6},{5,7},{6,4},{7,5},{8,10},{9,11},{10,... | collective-permute-start | bytes 1572872 | tf_op jit(solution)/shard_map/ppermute | solution.py:280
  6.2 0.3 collective-permute-start.5
  6.5 0.2 collective-permute-start
  6.6 1.4 %collective-permute-start.1 = (f32[2,32,2048]{2,1,0:T(8,128)S(1)}, f32[2,32,2048]{2,1,0:T(8,128)S(1)}, u32[]{:S(2)}, u32[]{:S(2)}) collective-permute-start(f32[2,32,2048]{2,1,0:T(8,128)S(1)} %get-tuple-element.15), channel_id=1, source_target_pairs={{0,2},{1,3},{2,0},{3,1},{4,6},{5,7},{6,4},{7,5},{8,10},{9,11},{10,... | collective-permute-start | bytes 1572872 | tf_op jit(solution)/shard_map/ppermute | solution.py:280
  8.0 0.0 collective-permute-done.3.x1
  8.0 0.6 collective-permute-start.2
  8.6 9.6 %collective-permute-done.4.x2 = f32[2,32,2048]{2,1,0:T(8,128)S(1)} collective-permute-done((f32[2,32,2048]{2,1,0:T(8,128)S(1)}, f32[2,32,2048]{2,1,0:T(8,128)S(1)}, u32[]{:S(2)}, u32[]{:S(2)}) %collective-permute-start.4) | collective-permute-done | bytes 524320 | tf_op jit(solution)/shard_map/ppermute | solution.py:280
  18.2 11.9 %collective-permute-done.5.x3 = f32[2,32,2048]{2,1,0:T(8,128)S(1)} collective-permute-done((f32[2,32,2048]{2,1,0:T(8,128)S(1)}, f32[2,32,2048]{2,1,0:T(8,128)S(1)}, u32[]{:S(2)}, u32[]{:S(2)}) %collective-permute-start.5) | collective-permute-done | bytes 524320 | tf_op jit(solution)/shard_map/ppermute | solution.py:280
  30.1 0.0 copy-done.5
  30.1 0.0 copy-done.6
  30.1 0.0 copy-done.7
  30.1 5.0 %columns.3 = f32[128,32,128]{2,1,0:T(8,128)} custom-call(s32[1]{0:T(128)} %bitcast.col_ref, f32[2,32,2048]{2,1,0:T(8,128)S(1)} %get-tuple-element.17.x0, f32[2,32,2048]{2,1,0:T(8,128)S(1)} %collective-permute-done.3.x1, f32[2,32,2048]{2,1,0:T(8,128)S(1)} %collective-permute-done.4.x2, f32[2,32,2048]{2,1,0:T(8,128)S(1)} %collective-permute-done.5.x3, ...), custom_call_target="tpu_custom_call" | custom-call | flops 805306368 | bytes 4194304 | tf_op jit(solution)/shard_map/columns/pallas_call | solution.py:173
  35.2 10.6 %all-to-all-start.1 = ((f32[128,32,128]{2,1,0:T(8,128)}), f32[128,32,128]{2,1,0:T(8,128)}, u32[]{:S(2)}, u32[]{:S(2)}) async-start(f32[128,32,128]{2,1,0:T(8,128)} %columns.3), calls=%async_computation.1 | async-start | bytes 4194304 | tf_op jit(solution)/shard_map/all_to_all | solution.py:284
  45.8 0.0 collective-permute-done.x1
  45.8 0.0 collective-permute-done.1.x2
  45.8 19.1 %collective-permute-done.2.x3 = f32[2,32,2048]{2,1,0:T(8,128)} collective-permute-done((f32[2,32,2048]{2,1,0:T(8,128)S(1)}, f32[2,32,2048]{2,1,0:T(8,128)}, u32[]{:S(2)}, u32[]{:S(2)}) %collective-permute-start.2) | collective-permute-done | bytes 524320 | tf_op jit(solution)/shard_map/ppermute | solution.py:280
  64.9 5.3 %columns.2 = f32[128,32,128]{2,1,0:T(8,128)S(1)} custom-call(s32[1]{0:T(128)} %bitcast.col_ref, f32[2,32,2048]{2,1,0:T(8,128)S(1)} %get-tuple-element.13.x0, f32[2,32,2048]{2,1,0:T(8,128)S(1)} %collective-permute-done.x1, f32[2,32,2048]{2,1,0:T(8,128)S(1)} %collective-permute-done.1.x2, f32[2,32,2048]{2,1,0:T(8,128)} %collective-permute-done.2.x3, ...), custom_call_target="tpu_custom_call" | custom-call | flops 206158430208 | bytes 4194304 | tf_op jit(solution)/shard_map/columns/pallas_call | solution.py:173
  70.2 0.0 copy-start
  70.2 1.3 %copy-done = f32[128,32,128]{2,1,0:T(8,128)} copy-done((f32[128,32,128]{2,1,0:T(8,128)}, f32[128,32,128]{2,1,0:T(8,128)S(1)}, u32[]{:S(2)}) %copy-start) | copy-done | bytes 2097176
  71.5 8.8 %all-to-all-done.1.c_ref = f32[128,32,128]{2,1,0:T(8,128)} async-done(((f32[128,32,128]{2,1,0:T(8,128)}), f32[128,32,128]{2,1,0:T(8,128)}, u32[]{:S(2)}, u32[]{:S(2)}) %all-to-all-start.1) | async-done | bytes 2097184 | tf_op jit(solution)/shard_map/all_to_all | solution.py:284
  80.4 6.3 %all-to-all-start = ((f32[128,32,128]{2,1,0:T(8,128)}), f32[128,32,128]{2,1,0:T(8,128)S(1)}, u32[]{:S(2)}, u32[]{:S(2)}) async-start(f32[128,32,128]{2,1,0:T(8,128)} %copy-done), calls=%async_computation | async-start | bytes 4194304 | tf_op jit(solution)/shard_map/all_to_all | solution.py:284
  86.7 0.0 copy-done.2
  86.7 0.0 copy-done.3
  86.7 0.0 copy-done.4
  86.7 9.9 %rows.2.rest_0_ = f32[2,64,8192]{2,1,0:T(8,128)} custom-call(f32[128,32,128]{2,1,0:T(8,128)} %all-to-all-done.1.c_ref, bf16[256,512]{1,0:T(8,128)(2,1)S(1)} %copy-done.3, bf16[256,512]{1,0:T(8,128)(2,1)S(1)} %copy-done.2, f32[32,8,128]{2,1,0:T(8,128)S(1)} %copy-done.4), custom_call_target="tpu_custom_call" | custom-call | flops 1610612736 | bytes 4194304 | tf_op jit(solution)/shard_map/rows/pallas_call | solution.py:253
  96.6 20.3 %all-to-all-done.c_ref = f32[128,32,128]{2,1,0:T(8,128)S(1)} async-done(((f32[128,32,128]{2,1,0:T(8,128)}), f32[128,32,128]{2,1,0:T(8,128)S(1)}, u32[]{:S(2)}, u32[]{:S(2)}) %all-to-all-start) | async-done | bytes 2097184 | tf_op jit(solution)/shard_map/all_to_all | solution.py:284
  116.9 8.3 %rows.3 = f32[2,64,8192]{2,1,0:T(8,128)} custom-call(f32[128,32,128]{2,1,0:T(8,128)S(1)} %all-to-all-done.c_ref, bf16[256,512]{1,0:T(8,128)(2,1)S(1)} %copy-done.3, bf16[256,512]{1,0:T(8,128)(2,1)S(1)} %copy-done.2, f32[32,8,128]{2,1,0:T(8,128)S(1)} %copy-done.4, f32[2,64,8192]{2,1,0:T(8,128)} %rows.2.rest_0_), custom_call_target="tpu_custom_call", output_to_operand_aliasing={{}: (4, {})} | custom-call | flops 1610612736 | bytes 4194304 | tf_op jit(solution)/shard_map/rows/pallas_call | solution.py:253
  (5 shorter events, 0.0 us)
Async XLA Ops:
  0.0 1.2 copy-start.1
  1.2 28.9 %copy-start.5 = (bf16[256,256]{1,0:T(8,128)(2,1)S(1)}, bf16[256,256]{1,0:T(8,128)(2,1)}, u32[]{:S(2)}) copy-start(bf16[256,256]{1,0:T(8,128)(2,1)} %constant.19.lo_ref) | copy-start | bytes 393220
  1.2 28.9 %copy-start.6 = (bf16[256,256]{1,0:T(8,128)(2,1)S(1)}, bf16[256,256]{1,0:T(8,128)(2,1)}, u32[]{:S(2)}) copy-start(bf16[256,256]{1,0:T(8,128)(2,1)} %constant.16.hi_ref) | copy-start | bytes 393220
  1.2 28.9 %copy-start.7 = (f32[128,128]{1,0:T(8,128)S(1)}, f32[128,128]{1,0:T(8,128)}, u32[]{:S(2)}) copy-start(f32[128,128]{1,0:T(8,128)} %constant.14.clone.twist_ref) | copy-start | bytes 196612
  3.3 4.8 %collective-permute-start.3 = (f32[2,32,2048]{2,1,0:T(8,128)S(1)}, f32[2,32,2048]{2,1,0:T(8,128)S(1)}, u32[]{:S(2)}, u32[]{:S(2)}) collective-permute-start(f32[2,32,2048]{2,1,0:T(8,128)S(1)} %get-tuple-element.18), channel_id=1, source_target_pairs={{0,1},{1,0},{2,3},{3,2},{4,5},{5,4},{6,7},{7,6},{8,9},{9,8},{10,11... | collective-permute-start | bytes 1572872 | tf_op jit(solution)/shard_map/ppermute | solution.py:280
  4.8 13.5 %collective-permute-start.4 = (f32[2,32,2048]{2,1,0:T(8,128)S(1)}, f32[2,32,2048]{2,1,0:T(8,128)S(1)}, u32[]{:S(2)}, u32[]{:S(2)}) collective-permute-start(f32[2,32,2048]{2,1,0:T(8,128)S(1)} %get-tuple-element.19), channel_id=1, source_target_pairs={{0,2},{1,3},{2,0},{3,1},{4,6},{5,7},{6,4},{7,5},{8,10},{9,11},{10,... | collective-permute-start | bytes 1572872 | tf_op jit(solution)/shard_map/ppermute | solution.py:280
  6.2 24.0 %collective-permute-start.5 = (f32[2,32,2048]{2,1,0:T(8,128)S(1)}, f32[2,32,2048]{2,1,0:T(8,128)S(1)}, u32[]{:S(2)}, u32[]{:S(2)}) collective-permute-start(f32[2,32,2048]{2,1,0:T(8,128)S(1)} %get-tuple-element.20), channel_id=1, source_target_pairs={{0,3},{1,2},{2,1},{3,0},{4,7},{5,6},{6,5},{7,4},{8,11},{9,10},{10,... | collective-permute-start | bytes 1572872 | tf_op jit(solution)/shard_map/ppermute | solution.py:280
  6.5 39.3 %collective-permute-start = (f32[2,32,2048]{2,1,0:T(8,128)S(1)}, f32[2,32,2048]{2,1,0:T(8,128)S(1)}, u32[]{:S(2)}, u32[]{:S(2)}) collective-permute-start(f32[2,32,2048]{2,1,0:T(8,128)S(1)} %get-tuple-element.14), channel_id=1, source_target_pairs={{0,1},{1,0},{2,3},{3,2},{4,5},{5,4},{6,7},{7,6},{8,9},{9,8},{10,11... | collective-permute-start | bytes 1572872 | tf_op jit(solution)/shard_map/ppermute | solution.py:280
  6.6 39.2 %collective-permute-start.1 = (f32[2,32,2048]{2,1,0:T(8,128)S(1)}, f32[2,32,2048]{2,1,0:T(8,128)S(1)}, u32[]{:S(2)}, u32[]{:S(2)}) collective-permute-start(f32[2,32,2048]{2,1,0:T(8,128)S(1)} %get-tuple-element.15), channel_id=1, source_target_pairs={{0,2},{1,3},{2,0},{3,1},{4,6},{5,7},{6,4},{7,5},{8,10},{9,11},{10,... | collective-permute-start | bytes 1572872 | tf_op jit(solution)/shard_map/ppermute | solution.py:280
  8.0 56.9 %collective-permute-start.2 = (f32[2,32,2048]{2,1,0:T(8,128)S(1)}, f32[2,32,2048]{2,1,0:T(8,128)}, u32[]{:S(2)}, u32[]{:S(2)}) collective-permute-start(f32[2,32,2048]{2,1,0:T(8,128)S(1)} %get-tuple-element.16), channel_id=1, source_target_pairs={{0,3},{1,2},{2,1},{3,0},{4,7},{5,6},{6,5},{7,4},{8,11},{9,10},{10,... | collective-permute-start | bytes 1572872 | tf_op jit(solution)/shard_map/ppermute | solution.py:280
  35.2 45.2 %all-to-all-start.1 = ((f32[128,32,128]{2,1,0:T(8,128)}), f32[128,32,128]{2,1,0:T(8,128)}, u32[]{:S(2)}, u32[]{:S(2)}) async-start(f32[128,32,128]{2,1,0:T(8,128)} %columns.3), calls=%async_computation.1 | async-start | bytes 4194304 | tf_op jit(solution)/shard_map/all_to_all | solution.py:284
  70.2 1.3 %copy-start = (f32[128,32,128]{2,1,0:T(8,128)}, f32[128,32,128]{2,1,0:T(8,128)S(1)}, u32[]{:S(2)}) copy-start(f32[128,32,128]{2,1,0:T(8,128)S(1)} %columns.2) | copy-start | bytes 6291460
  71.5 15.2 %copy-start.2 = (bf16[256,512]{1,0:T(8,128)(2,1)S(1)}, bf16[256,512]{1,0:T(8,128)(2,1)}, u32[]{:S(2)}) copy-start(bf16[256,512]{1,0:T(8,128)(2,1)} %constant.23.lo_ref) | copy-start | bytes 786436
  71.5 15.2 %copy-start.3 = (bf16[256,512]{1,0:T(8,128)(2,1)S(1)}, bf16[256,512]{1,0:T(8,128)(2,1)}, u32[]{:S(2)}) copy-start(bf16[256,512]{1,0:T(8,128)(2,1)} %constant.20.hi_ref) | copy-start | bytes 786436
  71.5 15.2 %copy-start.4 = (f32[32,8,128]{2,1,0:T(8,128)S(1)}, f32[32,8,128]{2,1,0:T(8,128)}, u32[]{:S(2)}) copy-start(f32[32,8,128]{2,1,0:T(8,128)} %constant.15.clone.twist_ref) | copy-start | bytes 393220
  80.4 36.5 %all-to-all-start = ((f32[128,32,128]{2,1,0:T(8,128)}), f32[128,32,128]{2,1,0:T(8,128)S(1)}, u32[]{:S(2)}, u32[]{:S(2)}) async-start(f32[128,32,128]{2,1,0:T(8,128)} %copy-done), calls=%async_computation | async-start | bytes 4194304 | tf_op jit(solution)/shard_map/all_to_all | solution.py:284

commit v3 on v2

--- a/solution.py
+++ b/solution.py
@@ -1,11 +1,14 @@
+import functools
+
 import numpy as np
 import jax
 import jax.numpy as jnp
 from jax import lax
 from jax.experimental import pallas as pl
 from jax.experimental.pallas import tpu as pltpu
-from jax.sharding import PartitionSpec as P
-
+from jax.sharding import Mesh, PartitionSpec as P
+
+PITCH = 72
 VMEM_LIMIT = 48 * 1024 * 1024
 
 
@@ -20,9 +23,14 @@
     return np.cos(ang), np.sin(ang)
 
 
+ROWS, COLS = ("y_hi", "x", "z"), ("y_lo", "core")
+ORDER_AXES = ("core", "z", "y_hi", "y_lo", "x")
+ORDER = np.arange(128).reshape(2, 4, 4, 2, 2).transpose(4, 2, 0, 3, 1).reshape(128)
+
+
 def lane_tables():
     step = np.arange(128)
-    cos, sin = unit(step[:, None] * step[None, :], 128)
+    cos, sin = unit(ORDER[:, None] * step[None, :], 128)
     matrix = np.block([[cos, -sin], [sin, cos]])
     cos, sin = unit(np.arange(64)[:, None] * step[None, :], 8192)
     twist = np.stack([cos, sin], 1).reshape(128, 128)
@@ -30,7 +38,7 @@
 
 
 def row_tables():
-    src = np.arange(128)
+    src = ORDER
     blocks = []
     for parity in (0, 1):
         cos, sin = unit(src[:, None] * (2 * np.arange(128) + parity)[None, :], 256)
@@ -101,30 +109,44 @@
     return hi, (x - hi.astype(jnp.float32)).astype(jnp.bfloat16)
 
 
-def spectrum_kernel(col_ref, noise_ref, root_ref, *outs):
-    for plane in range(2):
-        for d in range(4):
-            rows = pl.ds(pl.multiple_of((col_ref[0] ^ d) * 32, 32), 32)
-            root = root_ref[plane, rows, :].astype(jnp.float32)
-            for s in (0, 1):
-                outs[4 * plane + d][s] = noise_ref[s, plane, rows, :].astype(jnp.float32) * root
-
-
-def spectrum(col, noise, root):
+def spectrum_kernel(plane, partners, col_ref, noise_ref, root_ref, *rest):
+    outs, (noise, root, arrived) = rest[:len(partners)], rest[len(partners):]
+    copies = []
+    for i, d in enumerate(partners):
+        rows = pl.ds(pl.multiple_of((col_ref[0] ^ d) * 32, 32), 32)
+        copies.append([
+            pltpu.make_async_copy(noise_ref.at[0, plane, rows], noise.at[i, 0], arrived.at[i, 0]),
+            pltpu.make_async_copy(noise_ref.at[1, plane, rows], noise.at[i, 1], arrived.at[i, 1]),
+            pltpu.make_async_copy(root_ref.at[plane, rows], root.at[i], arrived.at[i, 2]),
+        ])
+        for copy in copies[-1]:
+            copy.start()
+    for i, out in enumerate(outs):
+        for copy in copies[i]:
+            copy.wait()
+        scale = root[i].astype(jnp.float32)
+        for s in (0, 1):
+            out[s] = noise[i, s].astype(jnp.float32) * scale
+
+
+def spectrum(col, noise, root, plane, partners, limit):
+    n = len(partners)
     return pl.pallas_call(
-        spectrum_kernel,
+        functools.partial(spectrum_kernel, plane, partners),
         grid_spec=pltpu.PrefetchScalarGridSpec(
             num_scalar_prefetch=1,
             grid=(1,),
-            in_specs=[
-                pl.BlockSpec((2, 2, 128, 2048), lambda i, c: (0, 0, 0, 0)),
-                pl.BlockSpec((2, 128, 2048), lambda i, c: (0, 0, 0)),
+            in_specs=[pl.BlockSpec(memory_space=pltpu.HBM)] * 2,
+            out_specs=[pl.BlockSpec((2, 32, 2048), lambda i, c: (0, 0, 0))] * n,
+            scratch_shapes=[
+                pltpu.VMEM((n, 2, 32, 2048), jnp.bfloat16),
+                pltpu.VMEM((n, 32, 2048), jnp.bfloat16),
+                pltpu.SemaphoreType.DMA((n, 3)),
             ],
-            out_specs=[pl.BlockSpec((2, 32, 2048), lambda i, c: (0, 0, 0))] * 8,
         ),
-        out_shape=[jax.ShapeDtypeStruct((2, 32, 2048), jnp.float32)] * 8,
-        compiler_params=pltpu.CompilerParams(vmem_limit_bytes=VMEM_LIMIT),
-        cost_estimate=pl.CostEstimate(flops=1 << 21, bytes_accessed=7 << 20, transcendentals=0),
+        out_shape=[jax.ShapeDtypeStruct((2, 32, 2048), jnp.float32)] * n,
+        compiler_params=pltpu.CompilerParams(vmem_limit_bytes=limit),
+        cost_estimate=pl.CostEstimate(flops=n << 18, bytes_accessed=n * (7 << 17), transcendentals=0),
         name="spectrum",
     )(col, noise, root)
 
@@ -153,12 +175,12 @@
             y_low = b + 8 * h
             value = cmul(value, twist_ref[2 * y_low:2 * y_low + 1, :], twist_ref[2 * y_low + 1:2 * y_low + 2, :])
             for s in (0, 1):
-                turned[s, pl.ds(y_low, 8, stride=64), :] = value[s]
+                turned[s, pl.ds(y_low, 8, stride=PITCH), :] = value[s]
     flat = out_ref.reshape(128 * 8, 128)
     dims = (((1,), (1,)), ((), ()))
     for half in range(2):
-        rows = slice(half * 256, half * 256 + 256)
-        hi, lo = parts(jnp.concatenate([turned[0, rows, :], turned[1, rows, :]], 1))
+        rows = [slice(k * PITCH, k * PITCH + 64) for k in range(4 * half, 4 * half + 4)]
+        hi, lo = parts(jnp.concatenate([jnp.concatenate([turned[s, r, :] for r in rows], 0) for s in (0, 1)], 1))
         result = lax.dot_general(hi_ref[...], hi, dims, preferred_element_type=jnp.float32)
         result += lax.dot_general(lo_ref[...], hi, dims, preferred_element_type=jnp.float32)
         result += lax.dot_general(hi_ref[...], lo, dims, preferred_element_type=jnp.float32)
@@ -184,7 +206,7 @@
             out_specs=pl.BlockSpec((128, 8, 128), lambda i, c: (0, i, 0)),
             scratch_shapes=[
                 pltpu.VMEM((2, 8, 8, 8, 128), jnp.float32),
-                pltpu.VMEM((2, 512, 128), jnp.float32),
+                pltpu.VMEM((2, 8 * PITCH, 128), jnp.float32),
             ],
         ),
         out_shape=jax.ShapeDtypeStruct((128, 32, 128), jnp.float32),
@@ -194,53 +216,55 @@
     )(col, *pieces, hi, lo, twist)
 
 
-def rows_kernel(c_ref, hi_ref, lo_ref, twist_ref, *rest):
-    out_ref, steps = rest[-2:]
+def rows_kernel(plane, c_ref, hi_ref, lo_ref, twist_ref, *rest):
+    out_ref, steps, ready, sent = rest[-4:]
     flat = c_ref.reshape(128 * 32, 128)
 
-    def one_pair(pair, _):
-        re = flat[pl.ds(2 * pair, 128, stride=32), :]
-        im = flat[pl.ds(2 * pair + 1, 128, stride=32), :]
-        both = jnp.concatenate([re.T, im.T], 1)
-        hi, lo = parts(both)
+    def some_pairs(step, _):
+        both = []
+        for t in range(8):
+            at = 2 * (8 * step + t)
+            both.append(jnp.concatenate([flat[pl.ds(at + s, 128, stride=32), :].T for s in (0, 1)], 1))
+        hi, lo = parts(jnp.concatenate(both, 0))
         result = jnp.dot(hi, hi_ref[...], preferred_element_type=jnp.float32)
         result += jnp.dot(hi, lo_ref[...], preferred_element_type=jnp.float32)
         result += jnp.dot(lo, hi_ref[...], preferred_element_type=jnp.float32)
-        for k in (0, 1):
-            rows = slice(64 * k, 64 * k + 64)
+        for t in range(16):
+            k = 16 * step + t
             for parity in (0, 1):
-                at = parity * 256
-                value = (result[rows, at:at + 128], result[rows, at + 128:at + 256])
-                value = cmul(
-                    value,
-                    twist_ref[2 * pair + k, 2 * parity:2 * parity + 1, :],
-                    twist_ref[2 * pair + k, 2 * parity + 1:2 * parity + 2, :],
-                )
-                for s in (0, 1):
-                    steps[2 * parity + s, 2 * pair + k] = value[s]
-        @pl.when(pair == 0)
-        def _():
-            steps[0, 0] -= im.T[0:64, 0:1] * (1.0 / 4096.0)
-            steps[2, 0] -= re.T[0:64, 0:1] * (1.0 / 4096.0)
+                re, im = (result[64 * t:64 * t + 64, at:at + 128] for at in (256 * parity, 256 * parity + 128))
+                twist = (twist_ref[k, j:j + 1, :] for j in (2 * parity, 2 * parity + 1))
+                for s, value in enumerate(cmul((re, im), *twist)):
+                    steps[2 * parity + s, k] = value
         return 0
 
-    lax.fori_loop(0, 16, one_pair, 0)
+    lax.fori_loop(0, 2, some_pairs, 0)
+    for s in (0, 1):
+        first = flat[pl.ds(s, 128, stride=32), :].T[0:64, 0:1] * (1.0 / 4096.0)
+        steps[2 - 2 * s, 0] -= first
+
+    def copy(group):
+        part = pl.ds(pl.multiple_of(group * 8, 8), 8)
+        return pltpu.make_async_copy(ready.at[part], out_ref.at[plane, part], sent.at[group])
 
     def one_group(group, _):
-        at = pl.multiple_of(group * 8, 8)
+        here = pl.ds(pl.multiple_of(group * 8, 8), 8)
         for parity in (0, 1):
             mid = [[None] * 8 for _ in range(4)]
             for low in range(8):
-                v = [tuple(steps[2 * parity + s, 8 * high + low, pl.ds(at, 8), :] for s in (0, 1)) for high in range(4)]
+                v = [tuple(steps[2 * parity + s, 8 * high + low, here, :] for s in (0, 1)) for high in range(4)]
                 for b, value in enumerate(dft4(v)):
                     mid[b][low] = const_mul(value, low * b, 32)
             for b in range(4):
                 for h, value in enumerate(dft8_real(mid[b])):
                     col = (parity * 32 + b + 4 * h) * 128
-                    out_ref[0, pl.ds(at, 8), col:col + 128] = value
+                    ready[here, col:col + 128] = value
+        copy(group).start()
         return 0
 
-    lax.fori_loop(0, 8, one_group, 0)
+    lax.fori_loop(0, 8, one_group, 0, unroll=True)
+    for group in range(8):
+        copy(group).wait()
 
 
 def rows(full, hi, lo, twist, plane, field=None):
@@ -251,12 +275,16 @@
         operands.append(field)
         specs.append(pl.BlockSpec(memory_space=pl.ANY))
     return pl.pallas_call(
-        rows_kernel,
+        functools.partial(rows_kernel, plane),
         grid=(1,),
         in_specs=specs,
-        out_specs=pl.BlockSpec((1, 64, 8192), lambda i: (plane, 0, 0)),
+        out_specs=pl.BlockSpec(memory_space=pl.ANY),
         out_shape=jax.ShapeDtypeStruct((2, 64, 8192), jnp.float32),
-        scratch_shapes=[pltpu.VMEM((4, 32, 64, 128), jnp.float32)],
+        scratch_shapes=[
+            pltpu.VMEM((4, 32, 64, 128), jnp.float32),
+            pltpu.VMEM((64, 8192), jnp.float32),
+            pltpu.SemaphoreType.DMA((8,)),
+        ],
         input_output_aliases={} if field is None else {4: 0},
         compiler_params=pltpu.CompilerParams(vmem_limit_bytes=VMEM_LIMIT),
         cost_estimate=pl.CostEstimate(flops=3 << 29, bytes_accessed=4 << 20, transcendentals=0),
@@ -269,29 +297,31 @@
     row_matrix, row_twist = row_tables()
     lane_hi, lane_lo = split_bf16(lane_matrix)
     row_hi, row_lo = split_bf16(row_matrix)
-    col = lax.axis_index("cols")[None]
+    col = lax.axis_index(COLS)[None]
     field = None
     full = []
-    sent = spectrum(col, noise, root)
-    got = [sent[0:4], sent[4:8]]
+    got = [[None] * 4 for _ in range(2)]
+    for plane, partners, limit in ((0, (2,), 60 << 20), (0, (3, 1, 0), VMEM_LIMIT), (1, (2, 3, 1, 0), VMEM_LIMIT)):
+        for d, piece in zip(partners, spectrum(col, noise, root, plane, partners, limit)):
+            got[plane][d] = piece
     for plane in range(2):
-        got[plane] = list(got[plane])
         for d in (2, 3, 1):
-            got[plane][d] = lax.ppermute(got[plane][d], "cols", [(c, c ^ d) for c in range(4)])
+            got[plane][d] = lax.ppermute(got[plane][d], COLS, [(c, c ^ d) for c in range(4)])
     for plane in range(2):
         pieces = got[plane]
         blocks = columns(col, pieces, lane_hi, lane_lo, jnp.asarray(lane_twist), 3 << (28 + 8 * plane))
-        full.append(lax.all_to_all(blocks, ("rows", "cols"), 0, 0, tiled=True))
+        full.append(lax.all_to_all(blocks, ORDER_AXES, 0, 0, tiled=True))
     for plane in range(2):
         field = rows(full[plane], row_hi, row_lo, jnp.asarray(row_twist), plane, field)
     return field
 
 
 def solution(mesh):
+    split = Mesh(mesh.devices.reshape(2, 4, 4, 2, 2), ROWS + COLS)
     return jax.shard_map(
         shards,
-        mesh=mesh,
-        in_specs=(P(None, None, "rows", "cols"), P(None, "rows", "cols")),
-        out_specs=P(None, ("rows", "cols"), None),
+        mesh=split,
+        in_specs=(P(None, None, ROWS, COLS), P(None, ROWS, COLS)),
+        out_specs=P(None, ROWS + COLS, None),
         check_vma=False,
     )

time: 126 us -> 118 us (0.937)
  waiting for transfers between devices: 69.7 us -> 63.2 us
  Pallas kernels: 30.5 us -> 25.7 us
  starting transfers between devices: 22.3 us -> 26.4 us
    ppermute x6, waiting for transfers between devices: 40.6 us -> 34.7 us  [shards(): lax.ppermute(got[plane][d], COLS, [(c, c ^ d) for c in range(4)])]
    ppermute x6, starting transfers between devices: 5.37 us -> 9.26 us  [shards(): lax.ppermute(got[plane][d], COLS, [(c, c ^ d) for c in range(4)])]
    pallas_call x2, Pallas kernels: 10.3 us -> 7.52 us  [columns(): pl.pallas_call(columns_kernel, grid_spec=pltpu.PrefetchScalarGridSpec(num...]
    pallas_call x3 -> x5, Pallas kernels: 20.3 us -> 18.2 us  [the longest x2 11 us: rows(): pl.pallas_call(functools.partial(rows_kernel, plane), grid=(1,), in_specs...]
    unnamed x16 -> x22, local copies, waits for them, and re-layouts: 2.56 us -> 2.13 us
where the time goes in v3:
time: 118 us
  waiting for transfers between devices  63.2 us (54%)
  starting transfers between devices  26.4 us (22%)
  Pallas kernels  25.7 us (22%)
  local copies, waits for them, and re-layouts  2.13 us (2%)
    ppermute x6, waiting for transfers between devices, shards(): lax.ppermute(got[plane][d], COLS, [(c, c ^ d) for c in range(4)])  34.7 us
    all_to_all x2, waiting for transfers between devices, shards(): full.append(lax.all_to_all(blocks, ORDER_AXES, 0, 0, tiled=True))  28.6 us
    all_to_all x2, starting transfers between devices, shards(): full.append(lax.all_to_all(blocks, ORDER_AXES, 0, 0, tiled=True))  17.1 us
    pallas_call x2, Pallas kernels, rows(): pl.pallas_call(functools.partial(rows_kernel, plane), grid=(1,), in_specs...  11 us
    ppermute x6, starting transfers between devices, shards(): lax.ppermute(got[plane][d], COLS, [(c, c ^ d) for c in range(4)])  9.26 us
    pallas_call x2, Pallas kernels, columns(): pl.pallas_call(columns_kernel, grid_spec=pltpu.PrefetchScalarGridSpec(num...  7.52 us
    pallas_call x3, Pallas kernels, spectrum(): pl.pallas_call(functools.partial(spectrum_kernel, plane, partners), grid_...  7.22 us
  transfers between devices with their start and end apart: 8, of which 5 were waited for; matrix products, arithmetic and copies ran while one was open for 0% of the time, Pallas kernels for 16%

profile of v3, /device:TPU:1, one launch (start us, length us, event | category | flops | bytes accessed | tf_op | source)
XLA Modules:
  0.0 117.6 jit_solution(13241591302909578749)
XLA Ops:
  0.0 2.0 %spectrum.5 = f32[2,32,2048]{2,1,0:T(8,128)} custom-call(s32[1]{0:T(128)} %bitcast.col_ref, bf16[2,2,128,2048]{3,2,1,0:T(8,128)(2,1)} %noise_ref.5, bf16[2,128,2048]{2,1,0:T(8,128)(2,1)} %root_ref.5), custom_call_target="tpu_custom_call" | custom-call | flops 262144 | bytes 917504 | tf_op jit(solution)/shard_map/spectrum/pallas_call | solution.py:134
  2.1 2.2 %collective-permute-start.4 = (f32[2,32,2048]{2,1,0:T(8,128)}, f32[2,32,2048]{2,1,0:T(8,128)S(1)}, u32[]{:S(2)}, u32[]{:S(2)}) collective-permute-start(f32[2,32,2048]{2,1,0:T(8,128)} %spectrum.5), channel_id=1, source_target_pairs={{0,2},{1,3},{2,0},{3,1},{4,6},{5,7},{6,4},{7,5},{8,10},{9,11},{10,... | collective-permute-start | bytes 1572872 | tf_op jit(solution)/shard_map/ppermute | solution.py:309
  4.3 0.0 copy-done.1
  4.3 0.0 copy-done
  4.3 1.8 %spectrum.4 = (f32[2,32,2048]{2,1,0:T(8,128)S(1)}, f32[2,32,2048]{2,1,0:T(8,128)S(1)}, f32[2,32,2048]{2,1,0:T(8,128)S(1)}) custom-call(s32[1]{0:T(128)} %bitcast.col_ref, bf16[2,2,128,2048]{3,2,1,0:T(8,128)(2,1)S(1)} %copy-done, bf16[2,128,2048]{2,1,0:T(8,128)(2,1)S(1)} %copy-done.1), custom_call_target="tpu_custom_call" | custom-call | flops 786432 | bytes 2752512 | tf_op jit(solution)/shard_map/spectrum/pallas_call | solution.py:134
  6.0 0.0 copy-start.6
  6.0 0.0 copy-start.7
  6.1 0.0 copy-start.8
  6.1 1.0 collective-permute-start.3
  7.1 0.1 collective-permute-start.5
  7.2 3.4 %spectrum.3 = (f32[2,32,2048]{2,1,0:T(8,128)}, f32[2,32,2048]{2,1,0:T(8,128)}, f32[2,32,2048]{2,1,0:T(8,128)}, f32[2,32,2048]{2,1,0:T(8,128)S(1)}) custom-call(s32[1]{0:T(128)} %bitcast.col_ref, bf16[2,2,128,2048]{3,2,1,0:T(8,128)(2,1)S(1)} %copy-done, bf16[2,128,2048]{2,1,0:T(8,128)(2,1)S(1)} %copy-done.1), custom_call_target="tpu_custom_call" | custom-call | flops 1048576 | bytes 3670016 | tf_op jit(solution)/shard_map/spectrum/pallas_call | solution.py:134
  10.6 0.0 copy-start.9
  10.6 0.8 copy-done.9
  11.4 0.4 collective-permute-start
  11.8 1.4 %collective-permute-start.1 = (f32[2,32,2048]{2,1,0:T(8,128)}, f32[2,32,2048]{2,1,0:T(8,128)S(1)}, u32[]{:S(2)}, u32[]{:S(2)}) collective-permute-start(f32[2,32,2048]{2,1,0:T(8,128)} %get-tuple-element.14), channel_id=1, source_target_pairs={{0,2},{1,3},{2,0},{3,1},{4,6},{5,7},{6,4},{7,5},{8,10},{9,11},{10,... | collective-permute-start | bytes 1572872 | tf_op jit(solution)/shard_map/ppermute | solution.py:309
  13.2 2.5 %collective-permute-done.4.x2 = f32[2,32,2048]{2,1,0:T(8,128)S(1)} collective-permute-done((f32[2,32,2048]{2,1,0:T(8,128)}, f32[2,32,2048]{2,1,0:T(8,128)S(1)}, u32[]{:S(2)}, u32[]{:S(2)}) %collective-permute-start.4) | collective-permute-done | bytes 524320 | tf_op jit(solution)/shard_map/ppermute | solution.py:309
  15.7 4.1 %collective-permute-start.2 = (f32[2,32,2048]{2,1,0:T(8,128)}, f32[2,32,2048]{2,1,0:T(8,128)S(1)}, u32[]{:S(2)}, u32[]{:S(2)}) collective-permute-start(f32[2,32,2048]{2,1,0:T(8,128)} %get-tuple-element.15), channel_id=1, source_target_pairs={{0,3},{1,2},{2,1},{3,0},{4,7},{5,6},{6,5},{7,4},{8,11},{9,10},{10,... | collective-permute-start | bytes 1572872 | tf_op jit(solution)/shard_map/ppermute | solution.py:309
  19.8 0.0 collective-permute-done.3.x1
  19.8 9.3 %collective-permute-done.5.x3 = f32[2,32,2048]{2,1,0:T(8,128)S(1)} collective-permute-done((f32[2,32,2048]{2,1,0:T(8,128)S(1)}, f32[2,32,2048]{2,1,0:T(8,128)S(1)}, u32[]{:S(2)}, u32[]{:S(2)}) %collective-permute-start.5) | collective-permute-done | bytes 524320 | tf_op jit(solution)/shard_map/ppermute | solution.py:309
  29.1 4.1 %columns.3 = f32[128,32,128]{2,1,0:T(8,128)} custom-call(s32[1]{0:T(128)} %bitcast.col_ref, f32[2,32,2048]{2,1,0:T(8,128)S(1)} %get-tuple-element.16.x0, f32[2,32,2048]{2,1,0:T(8,128)S(1)} %collective-permute-done.3.x1, f32[2,32,2048]{2,1,0:T(8,128)S(1)} %collective-permute-done.4.x2, f32[2,32,2048]{2,1,0:T(8,128)S(1)} %collective-permute-done.5.x3, ...), custom_call_target="tpu_custom_call" | custom-call | flops 805306368 | bytes 4194304 | tf_op jit(solution)/shard_map/columns/pallas_call | solution.py:195
  33.2 10.6 %all-to-all-start.1 = ((f32[128,32,128]{2,1,0:T(8,128)}), f32[128,32,128]{2,1,0:T(8,128)}, u32[]{:S(2)}, u32[]{:S(2)}) async-start(f32[128,32,128]{2,1,0:T(8,128)} %columns.3), calls=%async_computation.1 | async-start | bytes 4194304 | tf_op jit(solution)/shard_map/all_to_all | solution.py:313
  43.8 0.0 collective-permute-done.x1
  43.9 0.0 collective-permute-done.1.x2
  43.9 22.9 %collective-permute-done.2.x3 = f32[2,32,2048]{2,1,0:T(8,128)S(1)} collective-permute-done((f32[2,32,2048]{2,1,0:T(8,128)}, f32[2,32,2048]{2,1,0:T(8,128)S(1)}, u32[]{:S(2)}, u32[]{:S(2)}) %collective-permute-start.2) | collective-permute-done | bytes 524320 | tf_op jit(solution)/shard_map/ppermute | solution.py:309
  66.7 0.0 copy-done.10
  66.7 3.5 %columns.2 = f32[128,32,128]{2,1,0:T(8,128)S(1)} custom-call(s32[1]{0:T(128)} %bitcast.col_ref, f32[2,32,2048]{2,1,0:T(8,128)S(1)} %copy-done.10, f32[2,32,2048]{2,1,0:T(8,128)S(1)} %collective-permute-done.x1, f32[2,32,2048]{2,1,0:T(8,128)S(1)} %collective-permute-done.1.x2, f32[2,32,2048]{2,1,0:T(8,128)S(1)} %collective-permute-done.2.x3, ...), custom_call_target="tpu_custom_call" | custom-call | flops 206158430208 | bytes 4194304 | tf_op jit(solution)/shard_map/columns/pallas_call | solution.py:195
  70.2 1.3 %copy-done.2 = f32[128,32,128]{2,1,0:T(8,128)} copy-done((f32[128,32,128]{2,1,0:T(8,128)}, f32[128,32,128]{2,1,0:T(8,128)S(1)}, u32[]{:S(2)}) %copy-start.2) | copy-done | bytes 2097176
  71.5 6.3 %all-to-all-done.1.c_ref = f32[128,32,128]{2,1,0:T(8,128)} async-done(((f32[128,32,128]{2,1,0:T(8,128)}), f32[128,32,128]{2,1,0:T(8,128)}, u32[]{:S(2)}, u32[]{:S(2)}) %all-to-all-start.1) | async-done | bytes 2097184 | tf_op jit(solution)/shard_map/all_to_all | solution.py:313
  77.8 6.5 %all-to-all-start = ((f32[128,32,128]{2,1,0:T(8,128)}), f32[128,32,128]{2,1,0:T(8,128)S(1)}, u32[]{:S(2)}, u32[]{:S(2)}) async-start(f32[128,32,128]{2,1,0:T(8,128)} %copy-done.2), calls=%async_computation | async-start | bytes 4194304 | tf_op jit(solution)/shard_map/all_to_all | solution.py:313
  84.4 6.3 %rows.2.rest_0_ = f32[2,64,8192]{2,1,0:T(8,128)} custom-call(f32[128,32,128]{2,1,0:T(8,128)} %all-to-all-done.1.c_ref, bf16[256,512]{1,0:T(8,128)(2,1)S(1)} %copy-done.4, bf16[256,512]{1,0:T(8,128)(2,1)S(1)} %copy-done.3, f32[32,8,128]{2,1,0:T(8,128)S(1)} %copy-done.5), custom_call_target="tpu_custom_call" | custom-call | flops 1610612736 | bytes 4194304 | tf_op jit(solution)/shard_map/rows/pallas_call | solution.py:277
  90.7 22.3 %all-to-all-done.c_ref = f32[128,32,128]{2,1,0:T(8,128)S(1)} async-done(((f32[128,32,128]{2,1,0:T(8,128)}), f32[128,32,128]{2,1,0:T(8,128)S(1)}, u32[]{:S(2)}, u32[]{:S(2)}) %all-to-all-start) | async-done | bytes 2097184 | tf_op jit(solution)/shard_map/all_to_all | solution.py:313
  112.9 4.7 %rows.3 = f32[2,64,8192]{2,1,0:T(8,128)} custom-call(f32[128,32,128]{2,1,0:T(8,128)S(1)} %all-to-all-done.c_ref, bf16[256,512]{1,0:T(8,128)(2,1)S(1)} %copy-done.4, bf16[256,512]{1,0:T(8,128)(2,1)S(1)} %copy-done.3, f32[32,8,128]{2,1,0:T(8,128)S(1)} %copy-done.5, f32[2,64,8192]{2,1,0:T(8,128)} %rows.2.rest_0_), custom_call_target="tpu_custom_call", output_to_operand_aliasing={{}: (4, {})} | custom-call | flops 1610612736 | bytes 4194304 | tf_op jit(solution)/shard_map/rows/pallas_call | solution.py:277
  (13 shorter events, 0.0 us)
Async XLA Ops:
  0.0 4.3 %copy-start.1 = (bf16[2,128,2048]{2,1,0:T(8,128)(2,1)S(1)}, bf16[2,128,2048]{2,1,0:T(8,128)(2,1)}, u32[]{:S(2)}) copy-start(bf16[2,128,2048]{2,1,0:T(8,128)(2,1)} %root_ref.5) | copy-start | bytes 3145732
  0.0 4.3 %copy-start = (bf16[2,2,128,2048]{3,2,1,0:T(8,128)(2,1)S(1)}, bf16[2,2,128,2048]{3,2,1,0:T(8,128)(2,1)}, u32[]{:S(2)}) copy-start(bf16[2,2,128,2048]{3,2,1,0:T(8,128)(2,1)} %noise_ref.5) | copy-start | bytes 6291460
  2.1 13.7 %collective-permute-start.4 = (f32[2,32,2048]{2,1,0:T(8,128)}, f32[2,32,2048]{2,1,0:T(8,128)S(1)}, u32[]{:S(2)}, u32[]{:S(2)}) collective-permute-start(f32[2,32,2048]{2,1,0:T(8,128)} %spectrum.5), channel_id=1, source_target_pairs={{0,2},{1,3},{2,0},{3,1},{4,6},{5,7},{6,4},{7,5},{8,10},{9,11},{10,... | collective-permute-start | bytes 1572872 | tf_op jit(solution)/shard_map/ppermute | solution.py:309
  6.0 23.1 %copy-start.6 = (bf16[256,256]{1,0:T(8,128)(2,1)S(1)}, bf16[256,256]{1,0:T(8,128)(2,1)}, u32[]{:S(2)}) copy-start(bf16[256,256]{1,0:T(8,128)(2,1)} %constant.23.lo_ref) | copy-start | bytes 393220
  6.0 23.1 %copy-start.7 = (bf16[256,256]{1,0:T(8,128)(2,1)S(1)}, bf16[256,256]{1,0:T(8,128)(2,1)}, u32[]{:S(2)}) copy-start(bf16[256,256]{1,0:T(8,128)(2,1)} %constant.20.hi_ref) | copy-start | bytes 393220
  6.1 23.1 %copy-start.8 = (f32[128,128]{1,0:T(8,128)S(1)}, f32[128,128]{1,0:T(8,128)}, u32[]{:S(2)}) copy-start(f32[128,128]{1,0:T(8,128)} %constant.18.clone.twist_ref) | copy-start | bytes 196612
  6.1 13.8 %collective-permute-start.3 = (f32[2,32,2048]{2,1,0:T(8,128)S(1)}, f32[2,32,2048]{2,1,0:T(8,128)S(1)}, u32[]{:S(2)}, u32[]{:S(2)}) collective-permute-start(f32[2,32,2048]{2,1,0:T(8,128)S(1)} %get-tuple-element.17), channel_id=1, source_target_pairs={{0,1},{1,0},{2,3},{3,2},{4,5},{5,4},{6,7},{7,6},{8,9},{9,8},{10,11... | collective-permute-start | bytes 1572872 | tf_op jit(solution)/shard_map/ppermute | solution.py:309
  7.1 22.0 %collective-permute-start.5 = (f32[2,32,2048]{2,1,0:T(8,128)S(1)}, f32[2,32,2048]{2,1,0:T(8,128)S(1)}, u32[]{:S(2)}, u32[]{:S(2)}) collective-permute-start(f32[2,32,2048]{2,1,0:T(8,128)S(1)} %get-tuple-element.18), channel_id=1, source_target_pairs={{0,3},{1,2},{2,1},{3,0},{4,7},{5,6},{6,5},{7,4},{8,11},{9,10},{10,... | collective-permute-start | bytes 1572872 | tf_op jit(solution)/shard_map/ppermute | solution.py:309
  10.6 0.8 copy-start.9
  11.4 32.5 %collective-permute-start = (f32[2,32,2048]{2,1,0:T(8,128)}, f32[2,32,2048]{2,1,0:T(8,128)S(1)}, u32[]{:S(2)}, u32[]{:S(2)}) collective-permute-start(f32[2,32,2048]{2,1,0:T(8,128)} %get-tuple-element.13), channel_id=1, source_target_pairs={{0,1},{1,0},{2,3},{3,2},{4,5},{5,4},{6,7},{7,6},{8,9},{9,8},{10,11... | collective-permute-start | bytes 1572872 | tf_op jit(solution)/shard_map/ppermute | solution.py:309
  11.8 32.0 %collective-permute-start.1 = (f32[2,32,2048]{2,1,0:T(8,128)}, f32[2,32,2048]{2,1,0:T(8,128)S(1)}, u32[]{:S(2)}, u32[]{:S(2)}) collective-permute-start(f32[2,32,2048]{2,1,0:T(8,128)} %get-tuple-element.14), channel_id=1, source_target_pairs={{0,2},{1,3},{2,0},{3,1},{4,6},{5,7},{6,4},{7,5},{8,10},{9,11},{10,... | collective-permute-start | bytes 1572872 | tf_op jit(solution)/shard_map/ppermute | solution.py:309
  15.7 51.0 %collective-permute-start.2 = (f32[2,32,2048]{2,1,0:T(8,128)}, f32[2,32,2048]{2,1,0:T(8,128)S(1)}, u32[]{:S(2)}, u32[]{:S(2)}) collective-permute-start(f32[2,32,2048]{2,1,0:T(8,128)} %get-tuple-element.15), channel_id=1, source_target_pairs={{0,3},{1,2},{2,1},{3,0},{4,7},{5,6},{6,5},{7,4},{8,11},{9,10},{10,... | collective-permute-start | bytes 1572872 | tf_op jit(solution)/shard_map/ppermute | solution.py:309
  33.2 33.5 %copy-start.10 = (f32[2,32,2048]{2,1,0:T(8,128)S(1)}, f32[2,32,2048]{2,1,0:T(8,128)}, u32[]{:S(2)}) copy-start(f32[2,32,2048]{2,1,0:T(8,128)} %copy-done.9) | copy-start | bytes 1572868
  33.2 44.6 %all-to-all-start.1 = ((f32[128,32,128]{2,1,0:T(8,128)}), f32[128,32,128]{2,1,0:T(8,128)}, u32[]{:S(2)}, u32[]{:S(2)}) async-start(f32[128,32,128]{2,1,0:T(8,128)} %columns.3), calls=%async_computation.1 | async-start | bytes 4194304 | tf_op jit(solution)/shard_map/all_to_all | solution.py:313
  70.2 1.3 %copy-start.2 = (f32[128,32,128]{2,1,0:T(8,128)}, f32[128,32,128]{2,1,0:T(8,128)S(1)}, u32[]{:S(2)}) copy-start(f32[128,32,128]{2,1,0:T(8,128)S(1)} %columns.2) | copy-start | bytes 6291460
  71.5 12.8 %copy-start.3 = (bf16[256,512]{1,0:T(8,128)(2,1)S(1)}, bf16[256,512]{1,0:T(8,128)(2,1)}, u32[]{:S(2)}) copy-start(bf16[256,512]{1,0:T(8,128)(2,1)} %constant.27.lo_ref) | copy-start | bytes 786436
  71.5 12.8 %copy-start.4 = (bf16[256,512]{1,0:T(8,128)(2,1)S(1)}, bf16[256,512]{1,0:T(8,128)(2,1)}, u32[]{:S(2)}) copy-start(bf16[256,512]{1,0:T(8,128)(2,1)} %constant.24.hi_ref) | copy-start | bytes 786436
  71.5 12.8 %copy-start.5 = (f32[32,8,128]{2,1,0:T(8,128)S(1)}, f32[32,8,128]{2,1,0:T(8,128)}, u32[]{:S(2)}) copy-start(f32[32,8,128]{2,1,0:T(8,128)} %constant.19.clone.twist_ref) | copy-start | bytes 393220
  77.8 35.1 %all-to-all-start = ((f32[128,32,128]{2,1,0:T(8,128)}), f32[128,32,128]{2,1,0:T(8,128)S(1)}, u32[]{:S(2)}, u32[]{:S(2)}) async-start(f32[128,32,128]{2,1,0:T(8,128)} %copy-done.2), calls=%async_computation | async-start | bytes 4194304 | tf_op jit(solution)/shard_map/all_to_all | solution.py:313

commit v4 on v3

--- a/solution.py
+++ b/solution.py
@@ -9,6 +9,7 @@
 from jax.sharding import Mesh, PartitionSpec as P
 
 PITCH = 72
+FIRST = 59 << 20
 VMEM_LIMIT = 48 * 1024 * 1024
 
 
@@ -24,8 +25,8 @@
 
 
 ROWS, COLS = ("y_hi", "x", "z"), ("y_lo", "core")
-ORDER_AXES = ("core", "z", "y_hi", "y_lo", "x")
-ORDER = np.arange(128).reshape(2, 4, 4, 2, 2).transpose(4, 2, 0, 3, 1).reshape(128)
+ORDER_AXES = ("core", "z", "x", "y_hi", "y_lo")
+ORDER = np.arange(128).reshape(2, 4, 4, 2, 2).transpose(4, 2, 1, 0, 3).reshape(128)
 
 
 def lane_tables():
@@ -109,42 +110,46 @@
     return hi, (x - hi.astype(jnp.float32)).astype(jnp.bfloat16)
 
 
-def spectrum_kernel(plane, partners, col_ref, noise_ref, root_ref, *rest):
+def spectrum_kernel(spans, partners, col_ref, noise_ref, root_ref, *rest):
     outs, (noise, root, arrived) = rest[:len(partners)], rest[len(partners):]
     copies = []
     for i, d in enumerate(partners):
-        rows = pl.ds(pl.multiple_of((col_ref[0] ^ d) * 32, 32), 32)
-        copies.append([
-            pltpu.make_async_copy(noise_ref.at[0, plane, rows], noise.at[i, 0], arrived.at[i, 0]),
-            pltpu.make_async_copy(noise_ref.at[1, plane, rows], noise.at[i, 1], arrived.at[i, 1]),
-            pltpu.make_async_copy(root_ref.at[plane, rows], root.at[i], arrived.at[i, 2]),
-        ])
-        for copy in copies[-1]:
-            copy.start()
+        block = pl.multiple_of((col_ref[0] ^ d) * 32, 32)
+        at = 0
+        for j, (plane, first, count) in enumerate(spans):
+            rows, here = pl.ds(pl.multiple_of(block + first, 16), count), pl.ds(at, count)
+            copies += [
+                pltpu.make_async_copy(noise_ref.at[0, plane, rows], noise.at[i, 0, here], arrived.at[i, j, 0]),
+                pltpu.make_async_copy(noise_ref.at[1, plane, rows], noise.at[i, 1, here], arrived.at[i, j, 1]),
+                pltpu.make_async_copy(root_ref.at[plane, rows], root.at[i, here], arrived.at[i, j, 2]),
+            ]
+            at += count
+    for copy in copies:
+        copy.start()
     for i, out in enumerate(outs):
-        for copy in copies[i]:
+        for copy in copies[3 * len(spans) * i:3 * len(spans) * (i + 1)]:
             copy.wait()
         scale = root[i].astype(jnp.float32)
         for s in (0, 1):
             out[s] = noise[i, s].astype(jnp.float32) * scale
 
 
-def spectrum(col, noise, root, plane, partners, limit):
-    n = len(partners)
+def spectrum(col, noise, root, spans, partners, limit, first=False):
+    n, count = len(partners), sum(span[2] for span in spans)
     return pl.pallas_call(
-        functools.partial(spectrum_kernel, plane, partners),
+        functools.partial(spectrum_kernel, spans, partners),
         grid_spec=pltpu.PrefetchScalarGridSpec(
             num_scalar_prefetch=1,
             grid=(1,),
             in_specs=[pl.BlockSpec(memory_space=pltpu.HBM)] * 2,
-            out_specs=[pl.BlockSpec((2, 32, 2048), lambda i, c: (0, 0, 0))] * n,
+            out_specs=[pl.BlockSpec((2, count, 2048), lambda i, c: (0, 0, 0))] * n,
             scratch_shapes=[
-                pltpu.VMEM((n, 2, 32, 2048), jnp.bfloat16),
-                pltpu.VMEM((n, 32, 2048), jnp.bfloat16),
-                pltpu.SemaphoreType.DMA((n, 3)),
+                pltpu.VMEM((n, 2, count, 2048), jnp.bfloat16),
+                pltpu.VMEM((n, count, 2048), jnp.bfloat16),
+                pltpu.SemaphoreType.DMA((n, len(spans), 3)),
             ],
         ),
-        out_shape=[jax.ShapeDtypeStruct((2, 32, 2048), jnp.float32)] * n,
+        out_shape=[(pltpu.VMEM if first else jax.ShapeDtypeStruct)((2, count, 2048), jnp.float32)] * n,
         compiler_params=pltpu.CompilerParams(vmem_limit_bytes=limit),
         cost_estimate=pl.CostEstimate(flops=n << 18, bytes_accessed=n * (7 << 17), transcendentals=0),
         name="spectrum",
@@ -301,8 +306,9 @@
     field = None
     full = []
     got = [[None] * 4 for _ in range(2)]
-    for plane, partners, limit in ((0, (2,), 60 << 20), (0, (3, 1, 0), VMEM_LIMIT), (1, (2, 3, 1, 0), VMEM_LIMIT)):
-        for d, piece in zip(partners, spectrum(col, noise, root, plane, partners, limit)):
+    for plane, partners, limit in ((0, (2,), FIRST), (0, (3, 1, 0), VMEM_LIMIT), (1, (2, 3, 1, 0), VMEM_LIMIT)):
+        made = spectrum(col, noise, root, ((plane, 0, 32),), partners, limit, limit == FIRST)
+        for d, piece in zip(partners, made):
             got[plane][d] = piece
     for plane in range(2):
         for d in (2, 3, 1):

time: 118 us -> 116 us (0.983)
  starting transfers between devices: 26.4 us -> 25.1 us
    all_to_all x2, starting transfers between devices: 17.1 us -> 15.8 us  [shards(): full.append(lax.all_to_all(blocks, ORDER_AXES, 0, 0, tiled=True))]
where the time goes in v4:
time: 116 us
  waiting for transfers between devices  63.9 us (55%)
  starting transfers between devices  25.1 us (22%)
  Pallas kernels  24.9 us (21%)
  local copies, waits for them, and re-layouts  2.13 us (2%)
    ppermute x6, waiting for transfers between devices, shards(): lax.ppermute(got[plane][d], COLS, [(c, c ^ d) for c in range(4)])  35.1 us
    all_to_all x2, waiting for transfers between devices, shards(): full.append(lax.all_to_all(blocks, ORDER_AXES, 0, 0, tiled=True))  28.8 us
    all_to_all x2, starting transfers between devices, shards(): full.append(lax.all_to_all(blocks, ORDER_AXES, 0, 0, tiled=True))  15.8 us
    pallas_call x2, Pallas kernels, rows(): pl.pallas_call(functools.partial(rows_kernel, plane), grid=(1,), in_specs...  11 us
    ppermute x6, starting transfers between devices, shards(): lax.ppermute(got[plane][d], COLS, [(c, c ^ d) for c in range(4)])  9.26 us
    pallas_call x2, Pallas kernels, columns(): pl.pallas_call(columns_kernel, grid_spec=pltpu.PrefetchScalarGridSpec(num...  7.52 us
    pallas_call x3, Pallas kernels, spectrum(): pl.pallas_call(functools.partial(spectrum_kernel, spans, partners), grid_...  6.41 us
  transfers between devices with their start and end apart: 8, of which 5 were waited for; matrix products, arithmetic and copies ran while one was open for 0% of the time, Pallas kernels for 16%

profile of v4, /device:TPU:1, one launch (start us, length us, event | category | flops | bytes accessed | tf_op | source)
XLA Modules:
  0.0 116.1 jit_solution(8107692981253220356)
XLA Ops:
  0.0 1.3 %spectrum.5 = f32[2,32,2048]{2,1,0:T(8,128)S(1)} custom-call(s32[1]{0:T(128)} %bitcast.col_ref, bf16[2,2,128,2048]{3,2,1,0:T(8,128)(2,1)} %noise_ref.5, bf16[2,128,2048]{2,1,0:T(8,128)(2,1)} %root_ref.5), custom_call_target="tpu_custom_call" | custom-call | flops 262144 | bytes 917504 | tf_op jit(solution)/shard_map/spectrum/pallas_call | solution.py:139
  1.3 2.2 %collective-permute-start.4 = (f32[2,32,2048]{2,1,0:T(8,128)S(1)}, f32[2,32,2048]{2,1,0:T(8,128)S(1)}, u32[]{:S(2)}, u32[]{:S(2)}) collective-permute-start(f32[2,32,2048]{2,1,0:T(8,128)S(1)} %spectrum.5), channel_id=1, source_target_pairs={{0,2},{1,3},{2,0},{3,1},{4,6},{5,7},{6,4},{7,5},{8,10},{9,11},{10,... | collective-permute-start | bytes 1572872 | tf_op jit(solution)/shard_map/ppermute | solution.py:315
  3.5 0.0 copy-done
  3.5 1.8 %spectrum.4 = (f32[2,32,2048]{2,1,0:T(8,128)S(1)}, f32[2,32,2048]{2,1,0:T(8,128)S(1)}, f32[2,32,2048]{2,1,0:T(8,128)S(1)}) custom-call(s32[1]{0:T(128)} %bitcast.col_ref, bf16[2,2,128,2048]{3,2,1,0:T(8,128)(2,1)S(1)} %copy-done, bf16[2,128,2048]{2,1,0:T(8,128)(2,1)S(1)} %copy-done.1), custom_call_target="tpu_custom_call" | custom-call | flops 786432 | bytes 2752512 | tf_op jit(solution)/shard_map/spectrum/pallas_call | solution.py:139
  5.2 0.0 copy-start.6
  5.3 0.0 copy-start.7
  5.3 0.0 copy-start.8
  5.3 1.0 collective-permute-start.3
  6.3 0.4 collective-permute-start.5
  6.7 3.4 %spectrum.3 = (f32[2,32,2048]{2,1,0:T(8,128)}, f32[2,32,2048]{2,1,0:T(8,128)}, f32[2,32,2048]{2,1,0:T(8,128)}, f32[2,32,2048]{2,1,0:T(8,128)S(1)}) custom-call(s32[1]{0:T(128)} %bitcast.col_ref, bf16[2,2,128,2048]{3,2,1,0:T(8,128)(2,1)S(1)} %copy-done, bf16[2,128,2048]{2,1,0:T(8,128)(2,1)S(1)} %copy-done.1), custom_call_target="tpu_custom_call" | custom-call | flops 1048576 | bytes 3670016 | tf_op jit(solution)/shard_map/spectrum/pallas_call | solution.py:139
  10.2 0.8 copy-done.9
  11.0 0.4 collective-permute-start
  11.4 1.0 collective-permute-start.1
  12.4 2.3 %collective-permute-done.4.x2 = f32[2,32,2048]{2,1,0:T(8,128)S(1)} collective-permute-done((f32[2,32,2048]{2,1,0:T(8,128)S(1)}, f32[2,32,2048]{2,1,0:T(8,128)S(1)}, u32[]{:S(2)}, u32[]{:S(2)}) %collective-permute-start.4) | collective-permute-done | bytes 524320 | tf_op jit(solution)/shard_map/ppermute | solution.py:315
  14.7 4.1 %collective-permute-start.2 = (f32[2,32,2048]{2,1,0:T(8,128)}, f32[2,32,2048]{2,1,0:T(8,128)S(1)}, u32[]{:S(2)}, u32[]{:S(2)}) collective-permute-start(f32[2,32,2048]{2,1,0:T(8,128)} %get-tuple-element.15), channel_id=1, source_target_pairs={{0,3},{1,2},{2,1},{3,0},{4,7},{5,6},{6,5},{7,4},{8,11},{9,10},{10,... | collective-permute-start | bytes 1572872 | tf_op jit(solution)/shard_map/ppermute | solution.py:315
  18.8 0.0 collective-permute-done.3.x1
  18.8 9.3 %collective-permute-done.5.x3 = f32[2,32,2048]{2,1,0:T(8,128)S(1)} collective-permute-done((f32[2,32,2048]{2,1,0:T(8,128)S(1)}, f32[2,32,2048]{2,1,0:T(8,128)S(1)}, u32[]{:S(2)}, u32[]{:S(2)}) %collective-permute-start.5) | collective-permute-done | bytes 524320 | tf_op jit(solution)/shard_map/ppermute | solution.py:315
  28.1 4.1 %columns.3 = f32[128,32,128]{2,1,0:T(8,128)} custom-call(s32[1]{0:T(128)} %bitcast.col_ref, f32[2,32,2048]{2,1,0:T(8,128)S(1)} %get-tuple-element.16.x0, f32[2,32,2048]{2,1,0:T(8,128)S(1)} %collective-permute-done.3.x1, f32[2,32,2048]{2,1,0:T(8,128)S(1)} %collective-permute-done.4.x2, f32[2,32,2048]{2,1,0:T(8,128)S(1)} %collective-permute-done.5.x3, ...), custom_call_target="tpu_custom_call" | custom-call | flops 805306368 | bytes 4194304 | tf_op jit(solution)/shard_map/columns/pallas_call | solution.py:200
  32.2 10.6 %all-to-all-start.1 = ((f32[128,32,128]{2,1,0:T(8,128)}), f32[128,32,128]{2,1,0:T(8,128)}, u32[]{:S(2)}, u32[]{:S(2)}) async-start(f32[128,32,128]{2,1,0:T(8,128)} %columns.3), calls=%async_computation.1 | async-start | bytes 4194304 | tf_op jit(solution)/shard_map/all_to_all | solution.py:319
  42.9 0.0 collective-permute-done.x1
  42.9 0.0 collective-permute-done.1.x2
  42.9 23.5 %collective-permute-done.2.x3 = f32[2,32,2048]{2,1,0:T(8,128)S(1)} collective-permute-done((f32[2,32,2048]{2,1,0:T(8,128)}, f32[2,32,2048]{2,1,0:T(8,128)S(1)}, u32[]{:S(2)}, u32[]{:S(2)}) %collective-permute-start.2) | collective-permute-done | bytes 524320 | tf_op jit(solution)/shard_map/ppermute | solution.py:315
  66.3 0.0 copy-done.10
  66.3 3.5 %columns.2 = f32[128,32,128]{2,1,0:T(8,128)S(1)} custom-call(s32[1]{0:T(128)} %bitcast.col_ref, f32[2,32,2048]{2,1,0:T(8,128)S(1)} %copy-done.10, f32[2,32,2048]{2,1,0:T(8,128)S(1)} %collective-permute-done.x1, f32[2,32,2048]{2,1,0:T(8,128)S(1)} %collective-permute-done.1.x2, f32[2,32,2048]{2,1,0:T(8,128)S(1)} %collective-permute-done.2.x3, ...), custom_call_target="tpu_custom_call" | custom-call | flops 206158430208 | bytes 4194304 | tf_op jit(solution)/shard_map/columns/pallas_call | solution.py:200
  69.8 1.3 %copy-done.2 = f32[128,32,128]{2,1,0:T(8,128)} copy-done((f32[128,32,128]{2,1,0:T(8,128)}, f32[128,32,128]{2,1,0:T(8,128)S(1)}, u32[]{:S(2)}) %copy-start.2) | copy-done | bytes 2097176
  71.1 6.6 %all-to-all-done.1.c_ref = f32[128,32,128]{2,1,0:T(8,128)} async-done(((f32[128,32,128]{2,1,0:T(8,128)}), f32[128,32,128]{2,1,0:T(8,128)}, u32[]{:S(2)}, u32[]{:S(2)}) %all-to-all-start.1) | async-done | bytes 2097184 | tf_op jit(solution)/shard_map/all_to_all | solution.py:319
  77.7 5.2 %all-to-all-start = ((f32[128,32,128]{2,1,0:T(8,128)}), f32[128,32,128]{2,1,0:T(8,128)S(1)}, u32[]{:S(2)}, u32[]{:S(2)}) async-start(f32[128,32,128]{2,1,0:T(8,128)} %copy-done.2), calls=%async_computation | async-start | bytes 4194304 | tf_op jit(solution)/shard_map/all_to_all | solution.py:319
  82.9 0.0 copy-done.3
  82.9 0.0 copy-done.4
  82.9 6.3 %rows.2.rest_0_ = f32[2,64,8192]{2,1,0:T(8,128)} custom-call(f32[128,32,128]{2,1,0:T(8,128)} %all-to-all-done.1.c_ref, bf16[256,512]{1,0:T(8,128)(2,1)S(1)} %copy-done.4, bf16[256,512]{1,0:T(8,128)(2,1)S(1)} %copy-done.3, f32[32,8,128]{2,1,0:T(8,128)S(1)} %copy-done.5), custom_call_target="tpu_custom_call" | custom-call | flops 1610612736 | bytes 4194304 | tf_op jit(solution)/shard_map/rows/pallas_call | solution.py:282
  89.2 22.2 %all-to-all-done.c_ref = f32[128,32,128]{2,1,0:T(8,128)S(1)} async-done(((f32[128,32,128]{2,1,0:T(8,128)}), f32[128,32,128]{2,1,0:T(8,128)S(1)}, u32[]{:S(2)}, u32[]{:S(2)}) %all-to-all-start) | async-done | bytes 2097184 | tf_op jit(solution)/shard_map/all_to_all | solution.py:319
  111.4 4.7 %rows.3 = f32[2,64,8192]{2,1,0:T(8,128)} custom-call(f32[128,32,128]{2,1,0:T(8,128)S(1)} %all-to-all-done.c_ref, bf16[256,512]{1,0:T(8,128)(2,1)S(1)} %copy-done.4, bf16[256,512]{1,0:T(8,128)(2,1)S(1)} %copy-done.3, f32[32,8,128]{2,1,0:T(8,128)S(1)} %copy-done.5, f32[2,64,8192]{2,1,0:T(8,128)} %rows.2.rest_0_), custom_call_target="tpu_custom_call", output_to_operand_aliasing={{}: (4, {})} | custom-call | flops 1610612736 | bytes 4194304 | tf_op jit(solution)/shard_map/rows/pallas_call | solution.py:282
  (13 shorter events, 0.0 us)
Async XLA Ops:
  0.0 3.5 %copy-start.1 = (bf16[2,128,2048]{2,1,0:T(8,128)(2,1)S(1)}, bf16[2,128,2048]{2,1,0:T(8,128)(2,1)}, u32[]{:S(2)}) copy-start(bf16[2,128,2048]{2,1,0:T(8,128)(2,1)} %root_ref.5) | copy-start | bytes 3145732
  0.0 3.5 %copy-start = (bf16[2,2,128,2048]{3,2,1,0:T(8,128)(2,1)S(1)}, bf16[2,2,128,2048]{3,2,1,0:T(8,128)(2,1)}, u32[]{:S(2)}) copy-start(bf16[2,2,128,2048]{3,2,1,0:T(8,128)(2,1)} %noise_ref.5) | copy-start | bytes 6291460
  1.3 13.4 %collective-permute-start.4 = (f32[2,32,2048]{2,1,0:T(8,128)S(1)}, f32[2,32,2048]{2,1,0:T(8,128)S(1)}, u32[]{:S(2)}, u32[]{:S(2)}) collective-permute-start(f32[2,32,2048]{2,1,0:T(8,128)S(1)} %spectrum.5), channel_id=1, source_target_pairs={{0,2},{1,3},{2,0},{3,1},{4,6},{5,7},{6,4},{7,5},{8,10},{9,11},{10,... | collective-permute-start | bytes 1572872 | tf_op jit(solution)/shard_map/ppermute | solution.py:315
  5.2 22.9 %copy-start.6 = (bf16[256,256]{1,0:T(8,128)(2,1)S(1)}, bf16[256,256]{1,0:T(8,128)(2,1)}, u32[]{:S(2)}) copy-start(bf16[256,256]{1,0:T(8,128)(2,1)} %constant.23.lo_ref) | copy-start | bytes 393220
  5.3 22.9 %copy-start.7 = (bf16[256,256]{1,0:T(8,128)(2,1)S(1)}, bf16[256,256]{1,0:T(8,128)(2,1)}, u32[]{:S(2)}) copy-start(bf16[256,256]{1,0:T(8,128)(2,1)} %constant.20.hi_ref) | copy-start | bytes 393220
  5.3 22.9 %copy-start.8 = (f32[128,128]{1,0:T(8,128)S(1)}, f32[128,128]{1,0:T(8,128)}, u32[]{:S(2)}) copy-start(f32[128,128]{1,0:T(8,128)} %constant.18.clone.twist_ref) | copy-start | bytes 196612
  5.3 13.6 %collective-permute-start.3 = (f32[2,32,2048]{2,1,0:T(8,128)S(1)}, f32[2,32,2048]{2,1,0:T(8,128)S(1)}, u32[]{:S(2)}, u32[]{:S(2)}) collective-permute-start(f32[2,32,2048]{2,1,0:T(8,128)S(1)} %get-tuple-element.17), channel_id=1, source_target_pairs={{0,1},{1,0},{2,3},{3,2},{4,5},{5,4},{6,7},{7,6},{8,9},{9,8},{10,11... | collective-permute-start | bytes 1572872 | tf_op jit(solution)/shard_map/ppermute | solution.py:315
  6.3 21.8 %collective-permute-start.5 = (f32[2,32,2048]{2,1,0:T(8,128)S(1)}, f32[2,32,2048]{2,1,0:T(8,128)S(1)}, u32[]{:S(2)}, u32[]{:S(2)}) collective-permute-start(f32[2,32,2048]{2,1,0:T(8,128)S(1)} %get-tuple-element.18), channel_id=1, source_target_pairs={{0,3},{1,2},{2,1},{3,0},{4,7},{5,6},{6,5},{7,4},{8,11},{9,10},{10,... | collective-permute-start | bytes 1572872 | tf_op jit(solution)/shard_map/ppermute | solution.py:315
  10.2 0.8 copy-start.9
  11.0 31.9 %collective-permute-start = (f32[2,32,2048]{2,1,0:T(8,128)}, f32[2,32,2048]{2,1,0:T(8,128)S(1)}, u32[]{:S(2)}, u32[]{:S(2)}) collective-permute-start(f32[2,32,2048]{2,1,0:T(8,128)} %get-tuple-element.13), channel_id=1, source_target_pairs={{0,1},{1,0},{2,3},{3,2},{4,5},{5,4},{6,7},{7,6},{8,9},{9,8},{10,11... | collective-permute-start | bytes 1572872 | tf_op jit(solution)/shard_map/ppermute | solution.py:315
  11.4 31.5 %collective-permute-start.1 = (f32[2,32,2048]{2,1,0:T(8,128)}, f32[2,32,2048]{2,1,0:T(8,128)S(1)}, u32[]{:S(2)}, u32[]{:S(2)}) collective-permute-start(f32[2,32,2048]{2,1,0:T(8,128)} %get-tuple-element.14), channel_id=1, source_target_pairs={{0,2},{1,3},{2,0},{3,1},{4,6},{5,7},{6,4},{7,5},{8,10},{9,11},{10,... | collective-permute-start | bytes 1572872 | tf_op jit(solution)/shard_map/ppermute | solution.py:315
  14.7 51.6 %collective-permute-start.2 = (f32[2,32,2048]{2,1,0:T(8,128)}, f32[2,32,2048]{2,1,0:T(8,128)S(1)}, u32[]{:S(2)}, u32[]{:S(2)}) collective-permute-start(f32[2,32,2048]{2,1,0:T(8,128)} %get-tuple-element.15), channel_id=1, source_target_pairs={{0,3},{1,2},{2,1},{3,0},{4,7},{5,6},{6,5},{7,4},{8,11},{9,10},{10,... | collective-permute-start | bytes 1572872 | tf_op jit(solution)/shard_map/ppermute | solution.py:315
  32.2 34.1 %copy-start.10 = (f32[2,32,2048]{2,1,0:T(8,128)S(1)}, f32[2,32,2048]{2,1,0:T(8,128)}, u32[]{:S(2)}) copy-start(f32[2,32,2048]{2,1,0:T(8,128)} %copy-done.9) | copy-start | bytes 1572868
  32.2 45.5 %all-to-all-start.1 = ((f32[128,32,128]{2,1,0:T(8,128)}), f32[128,32,128]{2,1,0:T(8,128)}, u32[]{:S(2)}, u32[]{:S(2)}) async-start(f32[128,32,128]{2,1,0:T(8,128)} %columns.3), calls=%async_computation.1 | async-start | bytes 4194304 | tf_op jit(solution)/shard_map/all_to_all | solution.py:319
  69.8 1.3 %copy-start.2 = (f32[128,32,128]{2,1,0:T(8,128)}, f32[128,32,128]{2,1,0:T(8,128)S(1)}, u32[]{:S(2)}) copy-start(f32[128,32,128]{2,1,0:T(8,128)S(1)} %columns.2) | copy-start | bytes 6291460
  71.1 11.8 %copy-start.3 = (bf16[256,512]{1,0:T(8,128)(2,1)S(1)}, bf16[256,512]{1,0:T(8,128)(2,1)}, u32[]{:S(2)}) copy-start(bf16[256,512]{1,0:T(8,128)(2,1)} %constant.27.lo_ref) | copy-start | bytes 786436
  71.1 11.8 %copy-start.4 = (bf16[256,512]{1,0:T(8,128)(2,1)S(1)}, bf16[256,512]{1,0:T(8,128)(2,1)}, u32[]{:S(2)}) copy-start(bf16[256,512]{1,0:T(8,128)(2,1)} %constant.24.hi_ref) | copy-start | bytes 786436
  71.1 11.8 %copy-start.5 = (f32[32,8,128]{2,1,0:T(8,128)S(1)}, f32[32,8,128]{2,1,0:T(8,128)}, u32[]{:S(2)}) copy-start(f32[32,8,128]{2,1,0:T(8,128)} %constant.19.clone.twist_ref) | copy-start | bytes 393220
  77.7 33.8 %all-to-all-start = ((f32[128,32,128]{2,1,0:T(8,128)}), f32[128,32,128]{2,1,0:T(8,128)S(1)}, u32[]{:S(2)}, u32[]{:S(2)}) async-start(f32[128,32,128]{2,1,0:T(8,128)} %copy-done.2), calls=%async_computation | async-start | bytes 4194304 | tf_op jit(solution)/shard_map/all_to_all | solution.py:319

commit v5 on v4

--- a/solution.py
+++ b/solution.py
@@ -225,7 +225,7 @@
     out_ref, steps, ready, sent = rest[-4:]
     flat = c_ref.reshape(128 * 32, 128)
 
-    def some_pairs(step, _):
+    def some_pairs(step):
         both = []
         for t in range(8):
             at = 2 * (8 * step + t)
@@ -241,19 +241,19 @@
                 twist = (twist_ref[k, j:j + 1, :] for j in (2 * parity, 2 * parity + 1))
                 for s, value in enumerate(cmul((re, im), *twist)):
                     steps[2 * parity + s, k] = value
-        return 0
-
-    lax.fori_loop(0, 2, some_pairs, 0)
+
+    for step in range(2):
+        some_pairs(step)
     for s in (0, 1):
         first = flat[pl.ds(s, 128, stride=32), :].T[0:64, 0:1] * (1.0 / 4096.0)
         steps[2 - 2 * s, 0] -= first
 
     def copy(group):
-        part = pl.ds(pl.multiple_of(group * 8, 8), 8)
+        part = pl.ds(group * 8, 8)
         return pltpu.make_async_copy(ready.at[part], out_ref.at[plane, part], sent.at[group])
 
-    def one_group(group, _):
-        here = pl.ds(pl.multiple_of(group * 8, 8), 8)
+    def one_group(group):
+        here = pl.ds(group * 8, 8)
         for parity in (0, 1):
             mid = [[None] * 8 for _ in range(4)]
             for low in range(8):
@@ -265,9 +265,9 @@
                     col = (parity * 32 + b + 4 * h) * 128
                     ready[here, col:col + 128] = value
         copy(group).start()
-        return 0
-
-    lax.fori_loop(0, 8, one_group, 0, unroll=True)
+
+    for group in range(8):
+        one_group(group)
     for group in range(8):
         copy(group).wait()
 

time: 116 us -> 117 us (level)
  no operation moved by 1% of the time
where the time goes in v5:
time: 117 us; the launch traced here: 116 us
  waiting for transfers between devices  63.8 us (55%)
  starting transfers between devices  25.1 us (21%)
  Pallas kernels  25 us (21%)
  local copies, waits for them, and re-layouts  2.13 us (2%)
    ppermute x6, waiting for transfers between devices, shards(): lax.ppermute(got[plane][d], COLS, [(c, c ^ d) for c in range(4)])  35.1 us
    all_to_all x2, waiting for transfers between devices, shards(): full.append(lax.all_to_all(blocks, ORDER_AXES, 0, 0, tiled=True))  28.8 us
    all_to_all x2, starting transfers between devices, shards(): full.append(lax.all_to_all(blocks, ORDER_AXES, 0, 0, tiled=True))  15.8 us
    pallas_call x2, Pallas kernels, rows(): pl.pallas_call(functools.partial(rows_kernel, plane), grid=(1,), in_specs...  11.1 us
    ppermute x6, starting transfers between devices, shards(): lax.ppermute(got[plane][d], COLS, [(c, c ^ d) for c in range(4)])  9.26 us
    pallas_call x2, Pallas kernels, columns(): pl.pallas_call(columns_kernel, grid_spec=pltpu.PrefetchScalarGridSpec(num...  7.52 us
    pallas_call x3, Pallas kernels, spectrum(): pl.pallas_call(functools.partial(spectrum_kernel, spans, partners), grid_...  6.41 us
  transfers between devices with their start and end apart: 8, of which 5 were waited for; matrix products, arithmetic and copies ran while one was open for 0% of the time, Pallas kernels for 16%

profile of v5, /device:TPU:1, one launch (start us, length us, event | category | flops | bytes accessed | tf_op | source)
XLA Modules:
  0.0 116.2 jit_solution(17812149657872202318)
XLA Ops:
  0.0 1.3 %spectrum.5 = f32[2,32,2048]{2,1,0:T(8,128)S(1)} custom-call(s32[1]{0:T(128)} %bitcast.col_ref, bf16[2,2,128,2048]{3,2,1,0:T(8,128)(2,1)} %noise_ref.5, bf16[2,128,2048]{2,1,0:T(8,128)(2,1)} %root_ref.5), custom_call_target="tpu_custom_call" | custom-call | flops 262144 | bytes 917504 | tf_op jit(solution)/shard_map/spectrum/pallas_call | solution.py:139
  1.3 2.2 %collective-permute-start.4 = (f32[2,32,2048]{2,1,0:T(8,128)S(1)}, f32[2,32,2048]{2,1,0:T(8,128)S(1)}, u32[]{:S(2)}, u32[]{:S(2)}) collective-permute-start(f32[2,32,2048]{2,1,0:T(8,128)S(1)} %spectrum.5), channel_id=1, source_target_pairs={{0,2},{1,3},{2,0},{3,1},{4,6},{5,7},{6,4},{7,5},{8,10},{9,11},{10,... | collective-permute-start | bytes 1572872 | tf_op jit(solution)/shard_map/ppermute | solution.py:315
  3.5 0.0 copy-done.1
  3.5 0.0 copy-done
  3.5 1.8 %spectrum.4 = (f32[2,32,2048]{2,1,0:T(8,128)S(1)}, f32[2,32,2048]{2,1,0:T(8,128)S(1)}, f32[2,32,2048]{2,1,0:T(8,128)S(1)}) custom-call(s32[1]{0:T(128)} %bitcast.col_ref, bf16[2,2,128,2048]{3,2,1,0:T(8,128)(2,1)S(1)} %copy-done, bf16[2,128,2048]{2,1,0:T(8,128)(2,1)S(1)} %copy-done.1), custom_call_target="tpu_custom_call" | custom-call | flops 786432 | bytes 2752512 | tf_op jit(solution)/shard_map/spectrum/pallas_call | solution.py:139
  5.2 0.0 copy-start.6
  5.3 0.0 copy-start.7
  5.3 0.0 copy-start.8
  5.3 1.0 collective-permute-start.3
  6.3 0.4 collective-permute-start.5
  6.7 3.4 %spectrum.3 = (f32[2,32,2048]{2,1,0:T(8,128)}, f32[2,32,2048]{2,1,0:T(8,128)}, f32[2,32,2048]{2,1,0:T(8,128)}, f32[2,32,2048]{2,1,0:T(8,128)S(1)}) custom-call(s32[1]{0:T(128)} %bitcast.col_ref, bf16[2,2,128,2048]{3,2,1,0:T(8,128)(2,1)S(1)} %copy-done, bf16[2,128,2048]{2,1,0:T(8,128)(2,1)S(1)} %copy-done.1), custom_call_target="tpu_custom_call" | custom-call | flops 1048576 | bytes 3670016 | tf_op jit(solution)/shard_map/spectrum/pallas_call | solution.py:139
  10.2 0.8 copy-done.9
  11.0 0.4 collective-permute-start
  11.4 1.0 collective-permute-start.1
  12.4 2.3 %collective-permute-done.4.x2 = f32[2,32,2048]{2,1,0:T(8,128)S(1)} collective-permute-done((f32[2,32,2048]{2,1,0:T(8,128)S(1)}, f32[2,32,2048]{2,1,0:T(8,128)S(1)}, u32[]{:S(2)}, u32[]{:S(2)}) %collective-permute-start.4) | collective-permute-done | bytes 524320 | tf_op jit(solution)/shard_map/ppermute | solution.py:315
  14.7 4.1 %collective-permute-start.2 = (f32[2,32,2048]{2,1,0:T(8,128)}, f32[2,32,2048]{2,1,0:T(8,128)S(1)}, u32[]{:S(2)}, u32[]{:S(2)}) collective-permute-start(f32[2,32,2048]{2,1,0:T(8,128)} %get-tuple-element.15), channel_id=1, source_target_pairs={{0,3},{1,2},{2,1},{3,0},{4,7},{5,6},{6,5},{7,4},{8,11},{9,10},{10,... | collective-permute-start | bytes 1572872 | tf_op jit(solution)/shard_map/ppermute | solution.py:315
  18.8 0.0 collective-permute-done.3.x1
  18.8 9.3 %collective-permute-done.5.x3 = f32[2,32,2048]{2,1,0:T(8,128)S(1)} collective-permute-done((f32[2,32,2048]{2,1,0:T(8,128)S(1)}, f32[2,32,2048]{2,1,0:T(8,128)S(1)}, u32[]{:S(2)}, u32[]{:S(2)}) %collective-permute-start.5) | collective-permute-done | bytes 524320 | tf_op jit(solution)/shard_map/ppermute | solution.py:315
  28.1 0.0 copy-done.8
  28.1 4.1 %columns.3 = f32[128,32,128]{2,1,0:T(8,128)} custom-call(s32[1]{0:T(128)} %bitcast.col_ref, f32[2,32,2048]{2,1,0:T(8,128)S(1)} %get-tuple-element.16.x0, f32[2,32,2048]{2,1,0:T(8,128)S(1)} %collective-permute-done.3.x1, f32[2,32,2048]{2,1,0:T(8,128)S(1)} %collective-permute-done.4.x2, f32[2,32,2048]{2,1,0:T(8,128)S(1)} %collective-permute-done.5.x3, ...), custom_call_target="tpu_custom_call" | custom-call | flops 805306368 | bytes 4194304 | tf_op jit(solution)/shard_map/columns/pallas_call | solution.py:200
  32.2 10.6 %all-to-all-start.1 = ((f32[128,32,128]{2,1,0:T(8,128)}), f32[128,32,128]{2,1,0:T(8,128)}, u32[]{:S(2)}, u32[]{:S(2)}) async-start(f32[128,32,128]{2,1,0:T(8,128)} %columns.3), calls=%async_computation.1 | async-start | bytes 4194304 | tf_op jit(solution)/shard_map/all_to_all | solution.py:319
  42.9 0.0 collective-permute-done.x1
  42.9 0.0 collective-permute-done.1.x2
  42.9 23.5 %collective-permute-done.2.x3 = f32[2,32,2048]{2,1,0:T(8,128)S(1)} collective-permute-done((f32[2,32,2048]{2,1,0:T(8,128)}, f32[2,32,2048]{2,1,0:T(8,128)S(1)}, u32[]{:S(2)}, u32[]{:S(2)}) %collective-permute-start.2) | collective-permute-done | bytes 524320 | tf_op jit(solution)/shard_map/ppermute | solution.py:315
  66.3 3.5 %columns.2 = f32[128,32,128]{2,1,0:T(8,128)S(1)} custom-call(s32[1]{0:T(128)} %bitcast.col_ref, f32[2,32,2048]{2,1,0:T(8,128)S(1)} %copy-done.10, f32[2,32,2048]{2,1,0:T(8,128)S(1)} %collective-permute-done.x1, f32[2,32,2048]{2,1,0:T(8,128)S(1)} %collective-permute-done.1.x2, f32[2,32,2048]{2,1,0:T(8,128)S(1)} %collective-permute-done.2.x3, ...), custom_call_target="tpu_custom_call" | custom-call | flops 206158430208 | bytes 4194304 | tf_op jit(solution)/shard_map/columns/pallas_call | solution.py:200
  69.8 0.0 copy-start.2
  69.8 1.3 %copy-done.2 = f32[128,32,128]{2,1,0:T(8,128)} copy-done((f32[128,32,128]{2,1,0:T(8,128)}, f32[128,32,128]{2,1,0:T(8,128)S(1)}, u32[]{:S(2)}) %copy-start.2) | copy-done | bytes 2097176
  71.1 6.6 %all-to-all-done.1.c_ref = f32[128,32,128]{2,1,0:T(8,128)} async-done(((f32[128,32,128]{2,1,0:T(8,128)}), f32[128,32,128]{2,1,0:T(8,128)}, u32[]{:S(2)}, u32[]{:S(2)}) %all-to-all-start.1) | async-done | bytes 2097184 | tf_op jit(solution)/shard_map/all_to_all | solution.py:319
  77.7 5.2 %all-to-all-start = ((f32[128,32,128]{2,1,0:T(8,128)}), f32[128,32,128]{2,1,0:T(8,128)S(1)}, u32[]{:S(2)}, u32[]{:S(2)}) async-start(f32[128,32,128]{2,1,0:T(8,128)} %copy-done.2), calls=%async_computation | async-start | bytes 4194304 | tf_op jit(solution)/shard_map/all_to_all | solution.py:319
  82.9 6.3 %rows.2.rest_0_ = f32[2,64,8192]{2,1,0:T(8,128)} custom-call(f32[128,32,128]{2,1,0:T(8,128)} %all-to-all-done.1.c_ref, bf16[256,512]{1,0:T(8,128)(2,1)S(1)} %copy-done.4, bf16[256,512]{1,0:T(8,128)(2,1)S(1)} %copy-done.3, f32[32,8,128]{2,1,0:T(8,128)S(1)} %copy-done.5), custom_call_target="tpu_custom_call" | custom-call | flops 1610612736 | bytes 4194304 | tf_op jit(solution)/shard_map/rows/pallas_call | solution.py:282
  89.3 22.2 %all-to-all-done.c_ref = f32[128,32,128]{2,1,0:T(8,128)S(1)} async-done(((f32[128,32,128]{2,1,0:T(8,128)}), f32[128,32,128]{2,1,0:T(8,128)S(1)}, u32[]{:S(2)}, u32[]{:S(2)}) %all-to-all-start) | async-done | bytes 2097184 | tf_op jit(solution)/shard_map/all_to_all | solution.py:319
  111.4 4.7 %rows.3 = f32[2,64,8192]{2,1,0:T(8,128)} custom-call(f32[128,32,128]{2,1,0:T(8,128)S(1)} %all-to-all-done.c_ref, bf16[256,512]{1,0:T(8,128)(2,1)S(1)} %copy-done.4, bf16[256,512]{1,0:T(8,128)(2,1)S(1)} %copy-done.3, f32[32,8,128]{2,1,0:T(8,128)S(1)} %copy-done.5, f32[2,64,8192]{2,1,0:T(8,128)} %rows.2.rest_0_), custom_call_target="tpu_custom_call", output_to_operand_aliasing={{}: (4, {})} | custom-call | flops 1610612736 | bytes 4194304 | tf_op jit(solution)/shard_map/rows/pallas_call | solution.py:282
  (13 shorter events, 0.0 us)
Async XLA Ops:
  0.0 3.5 %copy-start.1 = (bf16[2,128,2048]{2,1,0:T(8,128)(2,1)S(1)}, bf16[2,128,2048]{2,1,0:T(8,128)(2,1)}, u32[]{:S(2)}) copy-start(bf16[2,128,2048]{2,1,0:T(8,128)(2,1)} %root_ref.5) | copy-start | bytes 3145732
  0.0 3.5 %copy-start = (bf16[2,2,128,2048]{3,2,1,0:T(8,128)(2,1)S(1)}, bf16[2,2,128,2048]{3,2,1,0:T(8,128)(2,1)}, u32[]{:S(2)}) copy-start(bf16[2,2,128,2048]{3,2,1,0:T(8,128)(2,1)} %noise_ref.5) | copy-start | bytes 6291460
  1.3 13.4 %collective-permute-start.4 = (f32[2,32,2048]{2,1,0:T(8,128)S(1)}, f32[2,32,2048]{2,1,0:T(8,128)S(1)}, u32[]{:S(2)}, u32[]{:S(2)}) collective-permute-start(f32[2,32,2048]{2,1,0:T(8,128)S(1)} %spectrum.5), channel_id=1, source_target_pairs={{0,2},{1,3},{2,0},{3,1},{4,6},{5,7},{6,4},{7,5},{8,10},{9,11},{10,... | collective-permute-start | bytes 1572872 | tf_op jit(solution)/shard_map/ppermute | solution.py:315
  5.2 22.9 %copy-start.6 = (bf16[256,256]{1,0:T(8,128)(2,1)S(1)}, bf16[256,256]{1,0:T(8,128)(2,1)}, u32[]{:S(2)}) copy-start(bf16[256,256]{1,0:T(8,128)(2,1)} %constant.23.lo_ref) | copy-start | bytes 393220
  5.3 22.9 %copy-start.7 = (bf16[256,256]{1,0:T(8,128)(2,1)S(1)}, bf16[256,256]{1,0:T(8,128)(2,1)}, u32[]{:S(2)}) copy-start(bf16[256,256]{1,0:T(8,128)(2,1)} %constant.20.hi_ref) | copy-start | bytes 393220
  5.3 22.9 %copy-start.8 = (f32[128,128]{1,0:T(8,128)S(1)}, f32[128,128]{1,0:T(8,128)}, u32[]{:S(2)}) copy-start(f32[128,128]{1,0:T(8,128)} %constant.18.clone.twist_ref) | copy-start | bytes 196612
  5.3 13.6 %collective-permute-start.3 = (f32[2,32,2048]{2,1,0:T(8,128)S(1)}, f32[2,32,2048]{2,1,0:T(8,128)S(1)}, u32[]{:S(2)}, u32[]{:S(2)}) collective-permute-start(f32[2,32,2048]{2,1,0:T(8,128)S(1)} %get-tuple-element.17), channel_id=1, source_target_pairs={{0,1},{1,0},{2,3},{3,2},{4,5},{5,4},{6,7},{7,6},{8,9},{9,8},{10,11... | collective-permute-start | bytes 1572872 | tf_op jit(solution)/shard_map/ppermute | solution.py:315
  6.3 21.8 %collective-permute-start.5 = (f32[2,32,2048]{2,1,0:T(8,128)S(1)}, f32[2,32,2048]{2,1,0:T(8,128)S(1)}, u32[]{:S(2)}, u32[]{:S(2)}) collective-permute-start(f32[2,32,2048]{2,1,0:T(8,128)S(1)} %get-tuple-element.18), channel_id=1, source_target_pairs={{0,3},{1,2},{2,1},{3,0},{4,7},{5,6},{6,5},{7,4},{8,11},{9,10},{10,... | collective-permute-start | bytes 1572872 | tf_op jit(solution)/shard_map/ppermute | solution.py:315
  10.2 0.8 copy-start.9
  11.0 31.9 %collective-permute-start = (f32[2,32,2048]{2,1,0:T(8,128)}, f32[2,32,2048]{2,1,0:T(8,128)S(1)}, u32[]{:S(2)}, u32[]{:S(2)}) collective-permute-start(f32[2,32,2048]{2,1,0:T(8,128)} %get-tuple-element.13), channel_id=1, source_target_pairs={{0,1},{1,0},{2,3},{3,2},{4,5},{5,4},{6,7},{7,6},{8,9},{9,8},{10,11... | collective-permute-start | bytes 1572872 | tf_op jit(solution)/shard_map/ppermute | solution.py:315
  11.4 31.5 %collective-permute-start.1 = (f32[2,32,2048]{2,1,0:T(8,128)}, f32[2,32,2048]{2,1,0:T(8,128)S(1)}, u32[]{:S(2)}, u32[]{:S(2)}) collective-permute-start(f32[2,32,2048]{2,1,0:T(8,128)} %get-tuple-element.14), channel_id=1, source_target_pairs={{0,2},{1,3},{2,0},{3,1},{4,6},{5,7},{6,4},{7,5},{8,10},{9,11},{10,... | collective-permute-start | bytes 1572872 | tf_op jit(solution)/shard_map/ppermute | solution.py:315
  14.7 51.6 %collective-permute-start.2 = (f32[2,32,2048]{2,1,0:T(8,128)}, f32[2,32,2048]{2,1,0:T(8,128)S(1)}, u32[]{:S(2)}, u32[]{:S(2)}) collective-permute-start(f32[2,32,2048]{2,1,0:T(8,128)} %get-tuple-element.15), channel_id=1, source_target_pairs={{0,3},{1,2},{2,1},{3,0},{4,7},{5,6},{6,5},{7,4},{8,11},{9,10},{10,... | collective-permute-start | bytes 1572872 | tf_op jit(solution)/shard_map/ppermute | solution.py:315
  32.2 34.1 %copy-start.10 = (f32[2,32,2048]{2,1,0:T(8,128)S(1)}, f32[2,32,2048]{2,1,0:T(8,128)}, u32[]{:S(2)}) copy-start(f32[2,32,2048]{2,1,0:T(8,128)} %copy-done.9) | copy-start | bytes 1572868
  32.2 45.5 %all-to-all-start.1 = ((f32[128,32,128]{2,1,0:T(8,128)}), f32[128,32,128]{2,1,0:T(8,128)}, u32[]{:S(2)}, u32[]{:S(2)}) async-start(f32[128,32,128]{2,1,0:T(8,128)} %columns.3), calls=%async_computation.1 | async-start | bytes 4194304 | tf_op jit(solution)/shard_map/all_to_all | solution.py:319
  69.8 1.3 %copy-start.2 = (f32[128,32,128]{2,1,0:T(8,128)}, f32[128,32,128]{2,1,0:T(8,128)S(1)}, u32[]{:S(2)}) copy-start(f32[128,32,128]{2,1,0:T(8,128)S(1)} %columns.2) | copy-start | bytes 6291460
  71.1 11.8 %copy-start.3 = (bf16[256,512]{1,0:T(8,128)(2,1)S(1)}, bf16[256,512]{1,0:T(8,128)(2,1)}, u32[]{:S(2)}) copy-start(bf16[256,512]{1,0:T(8,128)(2,1)} %constant.27.lo_ref) | copy-start | bytes 786436
  71.1 11.8 %copy-start.4 = (bf16[256,512]{1,0:T(8,128)(2,1)S(1)}, bf16[256,512]{1,0:T(8,128)(2,1)}, u32[]{:S(2)}) copy-start(bf16[256,512]{1,0:T(8,128)(2,1)} %constant.24.hi_ref) | copy-start | bytes 786436
  71.1 11.8 %copy-start.5 = (f32[32,8,128]{2,1,0:T(8,128)S(1)}, f32[32,8,128]{2,1,0:T(8,128)}, u32[]{:S(2)}) copy-start(f32[32,8,128]{2,1,0:T(8,128)} %constant.19.clone.twist_ref) | copy-start | bytes 393220
  77.7 33.8 %all-to-all-start = ((f32[128,32,128]{2,1,0:T(8,128)}), f32[128,32,128]{2,1,0:T(8,128)S(1)}, u32[]{:S(2)}, u32[]{:S(2)}) async-start(f32[128,32,128]{2,1,0:T(8,128)} %copy-done.2), calls=%async_computation | async-start | bytes 4194304 | tf_op jit(solution)/shard_map/all_to_all | solution.py:319

commit v6 on v5

--- a/solution.py
+++ b/solution.py
@@ -25,8 +25,8 @@
 
 
 ROWS, COLS = ("y_hi", "x", "z"), ("y_lo", "core")
-ORDER_AXES = ("core", "z", "x", "y_hi", "y_lo")
-ORDER = np.arange(128).reshape(2, 4, 4, 2, 2).transpose(4, 2, 1, 0, 3).reshape(128)
+ORDER_AXES = ("core", "z", "x", "y_lo", "y_hi")
+ORDER = np.arange(128).reshape(2, 4, 4, 2, 2).transpose(4, 2, 1, 3, 0).reshape(128)
 
 
 def lane_tables():

time: 117 us -> 117 us (level)
    all_to_all x2, waiting for transfers between devices: 28.8 us -> 31.1 us  [shards(): full.append(lax.all_to_all(blocks, ORDER_AXES, 0, 0, tiled=True))]
    ppermute x6, waiting for transfers between devices: 35.1 us -> 33.3 us  [shards(): lax.ppermute(got[plane][d], COLS, [(c, c ^ d) for c in range(4)])]
where the time goes in v6:
time: 117 us
  waiting for transfers between devices  64.4 us (55%)
  starting transfers between devices  25.2 us (22%)
  Pallas kernels  25 us (21%)
  local copies, waits for them, and re-layouts  2.13 us (2%)
    ppermute x6, waiting for transfers between devices, shards(): lax.ppermute(got[plane][d], COLS, [(c, c ^ d) for c in range(4)])  33.3 us
    all_to_all x2, waiting for transfers between devices, shards(): full.append(lax.all_to_all(blocks, ORDER_AXES, 0, 0, tiled=True))  31.1 us
    all_to_all x2, starting transfers between devices, shards(): full.append(lax.all_to_all(blocks, ORDER_AXES, 0, 0, tiled=True))  15.9 us
    pallas_call x2, Pallas kernels, rows(): pl.pallas_call(functools.partial(rows_kernel, plane), grid=(1,), in_specs...  11.1 us
    ppermute x6, starting transfers between devices, shards(): lax.ppermute(got[plane][d], COLS, [(c, c ^ d) for c in range(4)])  9.26 us
    pallas_call x2, Pallas kernels, columns(): pl.pallas_call(columns_kernel, grid_spec=pltpu.PrefetchScalarGridSpec(num...  7.51 us
    pallas_call x3, Pallas kernels, spectrum(): pl.pallas_call(functools.partial(spectrum_kernel, spans, partners), grid_...  6.41 us
  transfers between devices with their start and end apart: 8, of which 5 were waited for; matrix products, arithmetic and copies ran while one was open for 0% of the time, Pallas kernels for 16%

profile of v6, /device:TPU:1, one launch (start us, length us, event | category | flops | bytes accessed | tf_op | source)
XLA Modules:
  0.0 116.9 jit_solution(12392322582149135193)
XLA Ops:
  0.0 1.3 %spectrum.5 = f32[2,32,2048]{2,1,0:T(8,128)S(1)} custom-call(s32[1]{0:T(128)} %bitcast.col_ref, bf16[2,2,128,2048]{3,2,1,0:T(8,128)(2,1)} %noise_ref.5, bf16[2,128,2048]{2,1,0:T(8,128)(2,1)} %root_ref.5), custom_call_target="tpu_custom_call" | custom-call | flops 262144 | bytes 917504 | tf_op jit(solution)/shard_map/spectrum/pallas_call | solution.py:139
  1.3 2.2 %collective-permute-start.4 = (f32[2,32,2048]{2,1,0:T(8,128)S(1)}, f32[2,32,2048]{2,1,0:T(8,128)S(1)}, u32[]{:S(2)}, u32[]{:S(2)}) collective-permute-start(f32[2,32,2048]{2,1,0:T(8,128)S(1)} %spectrum.5), channel_id=1, source_target_pairs={{0,2},{1,3},{2,0},{3,1},{4,6},{5,7},{6,4},{7,5},{8,10},{9,11},{10,... | collective-permute-start | bytes 1572872 | tf_op jit(solution)/shard_map/ppermute | solution.py:315
  3.5 1.8 %spectrum.4 = (f32[2,32,2048]{2,1,0:T(8,128)S(1)}, f32[2,32,2048]{2,1,0:T(8,128)S(1)}, f32[2,32,2048]{2,1,0:T(8,128)S(1)}) custom-call(s32[1]{0:T(128)} %bitcast.col_ref, bf16[2,2,128,2048]{3,2,1,0:T(8,128)(2,1)S(1)} %copy-done, bf16[2,128,2048]{2,1,0:T(8,128)(2,1)S(1)} %copy-done.1), custom_call_target="tpu_custom_call" | custom-call | flops 786432 | bytes 2752512 | tf_op jit(solution)/shard_map/spectrum/pallas_call | solution.py:139
  5.2 0.0 copy-start.6
  5.3 0.0 copy-start.7
  5.3 0.0 copy-start.8
  5.3 1.0 collective-permute-start.3
  6.3 0.4 collective-permute-start.5
  6.7 3.4 %spectrum.3 = (f32[2,32,2048]{2,1,0:T(8,128)}, f32[2,32,2048]{2,1,0:T(8,128)}, f32[2,32,2048]{2,1,0:T(8,128)}, f32[2,32,2048]{2,1,0:T(8,128)S(1)}) custom-call(s32[1]{0:T(128)} %bitcast.col_ref, bf16[2,2,128,2048]{3,2,1,0:T(8,128)(2,1)S(1)} %copy-done, bf16[2,128,2048]{2,1,0:T(8,128)(2,1)S(1)} %copy-done.1), custom_call_target="tpu_custom_call" | custom-call | flops 1048576 | bytes 3670016 | tf_op jit(solution)/shard_map/spectrum/pallas_call | solution.py:139
  10.2 0.0 copy-start.9
  10.2 0.8 copy-done.9
  11.0 0.4 collective-permute-start
  11.4 1.0 collective-permute-start.1
  12.4 2.3 %collective-permute-done.4.x2 = f32[2,32,2048]{2,1,0:T(8,128)S(1)} collective-permute-done((f32[2,32,2048]{2,1,0:T(8,128)S(1)}, f32[2,32,2048]{2,1,0:T(8,128)S(1)}, u32[]{:S(2)}, u32[]{:S(2)}) %collective-permute-start.4) | collective-permute-done | bytes 524320 | tf_op jit(solution)/shard_map/ppermute | solution.py:315
  14.7 4.1 %collective-permute-start.2 = (f32[2,32,2048]{2,1,0:T(8,128)}, f32[2,32,2048]{2,1,0:T(8,128)S(1)}, u32[]{:S(2)}, u32[]{:S(2)}) collective-permute-start(f32[2,32,2048]{2,1,0:T(8,128)} %get-tuple-element.15), channel_id=1, source_target_pairs={{0,3},{1,2},{2,1},{3,0},{4,7},{5,6},{6,5},{7,4},{8,11},{9,10},{10,... | collective-permute-start | bytes 1572872 | tf_op jit(solution)/shard_map/ppermute | solution.py:315
  18.8 0.0 collective-permute-done.3.x1
  18.8 9.3 %collective-permute-done.5.x3 = f32[2,32,2048]{2,1,0:T(8,128)S(1)} collective-permute-done((f32[2,32,2048]{2,1,0:T(8,128)S(1)}, f32[2,32,2048]{2,1,0:T(8,128)S(1)}, u32[]{:S(2)}, u32[]{:S(2)}) %collective-permute-start.5) | collective-permute-done | bytes 524320 | tf_op jit(solution)/shard_map/ppermute | solution.py:315
  28.1 0.0 copy-done.7
  28.1 4.1 %columns.3 = f32[128,32,128]{2,1,0:T(8,128)} custom-call(s32[1]{0:T(128)} %bitcast.col_ref, f32[2,32,2048]{2,1,0:T(8,128)S(1)} %get-tuple-element.16.x0, f32[2,32,2048]{2,1,0:T(8,128)S(1)} %collective-permute-done.3.x1, f32[2,32,2048]{2,1,0:T(8,128)S(1)} %collective-permute-done.4.x2, f32[2,32,2048]{2,1,0:T(8,128)S(1)} %collective-permute-done.5.x3, ...), custom_call_target="tpu_custom_call" | custom-call | flops 805306368 | bytes 4194304 | tf_op jit(solution)/shard_map/columns/pallas_call | solution.py:200
  32.2 10.6 %all-to-all-start.1 = ((f32[128,32,128]{2,1,0:T(8,128)}), f32[128,32,128]{2,1,0:T(8,128)}, u32[]{:S(2)}, u32[]{:S(2)}) async-start(f32[128,32,128]{2,1,0:T(8,128)} %columns.3), calls=%async_computation.1 | async-start | bytes 4194304 | tf_op jit(solution)/shard_map/all_to_all | solution.py:319
  42.9 0.0 collective-permute-done.x1
  42.9 0.0 collective-permute-done.1.x2
  42.9 21.7 %collective-permute-done.2.x3 = f32[2,32,2048]{2,1,0:T(8,128)S(1)} collective-permute-done((f32[2,32,2048]{2,1,0:T(8,128)}, f32[2,32,2048]{2,1,0:T(8,128)S(1)}, u32[]{:S(2)}, u32[]{:S(2)}) %collective-permute-start.2) | collective-permute-done | bytes 524320 | tf_op jit(solution)/shard_map/ppermute | solution.py:315
  64.6 0.0 copy-done.10
  64.6 3.5 %columns.2 = f32[128,32,128]{2,1,0:T(8,128)S(1)} custom-call(s32[1]{0:T(128)} %bitcast.col_ref, f32[2,32,2048]{2,1,0:T(8,128)S(1)} %copy-done.10, f32[2,32,2048]{2,1,0:T(8,128)S(1)} %collective-permute-done.x1, f32[2,32,2048]{2,1,0:T(8,128)S(1)} %collective-permute-done.1.x2, f32[2,32,2048]{2,1,0:T(8,128)S(1)} %collective-permute-done.2.x3, ...), custom_call_target="tpu_custom_call" | custom-call | flops 206158430208 | bytes 4194304 | tf_op jit(solution)/shard_map/columns/pallas_call | solution.py:200
  68.1 1.3 %copy-done.2 = f32[128,32,128]{2,1,0:T(8,128)} copy-done((f32[128,32,128]{2,1,0:T(8,128)}, f32[128,32,128]{2,1,0:T(8,128)S(1)}, u32[]{:S(2)}) %copy-start.2) | copy-done | bytes 2097176
  69.3 8.3 %all-to-all-done.1.c_ref = f32[128,32,128]{2,1,0:T(8,128)} async-done(((f32[128,32,128]{2,1,0:T(8,128)}), f32[128,32,128]{2,1,0:T(8,128)}, u32[]{:S(2)}, u32[]{:S(2)}) %all-to-all-start.1) | async-done | bytes 2097184 | tf_op jit(solution)/shard_map/all_to_all | solution.py:319
  77.7 5.3 %all-to-all-start = ((f32[128,32,128]{2,1,0:T(8,128)}), f32[128,32,128]{2,1,0:T(8,128)S(1)}, u32[]{:S(2)}, u32[]{:S(2)}) async-start(f32[128,32,128]{2,1,0:T(8,128)} %copy-done.2), calls=%async_computation | async-start | bytes 4194304 | tf_op jit(solution)/shard_map/all_to_all | solution.py:319
  83.0 0.0 copy-done.3
  83.0 6.3 %rows.2.rest_0_ = f32[2,64,8192]{2,1,0:T(8,128)} custom-call(f32[128,32,128]{2,1,0:T(8,128)} %all-to-all-done.1.c_ref, bf16[256,512]{1,0:T(8,128)(2,1)S(1)} %copy-done.4, bf16[256,512]{1,0:T(8,128)(2,1)S(1)} %copy-done.3, f32[32,8,128]{2,1,0:T(8,128)S(1)} %copy-done.5), custom_call_target="tpu_custom_call" | custom-call | flops 1610612736 | bytes 4194304 | tf_op jit(solution)/shard_map/rows/pallas_call | solution.py:282
  89.3 22.8 %all-to-all-done.c_ref = f32[128,32,128]{2,1,0:T(8,128)S(1)} async-done(((f32[128,32,128]{2,1,0:T(8,128)}), f32[128,32,128]{2,1,0:T(8,128)S(1)}, u32[]{:S(2)}, u32[]{:S(2)}) %all-to-all-start) | async-done | bytes 2097184 | tf_op jit(solution)/shard_map/all_to_all | solution.py:319
  112.1 4.8 %rows.3 = f32[2,64,8192]{2,1,0:T(8,128)} custom-call(f32[128,32,128]{2,1,0:T(8,128)S(1)} %all-to-all-done.c_ref, bf16[256,512]{1,0:T(8,128)(2,1)S(1)} %copy-done.4, bf16[256,512]{1,0:T(8,128)(2,1)S(1)} %copy-done.3, f32[32,8,128]{2,1,0:T(8,128)S(1)} %copy-done.5, f32[2,64,8192]{2,1,0:T(8,128)} %rows.2.rest_0_), custom_call_target="tpu_custom_call", output_to_operand_aliasing={{}: (4, {})} | custom-call | flops 1610612736 | bytes 4194304 | tf_op jit(solution)/shard_map/rows/pallas_call | solution.py:282
  (13 shorter events, 0.0 us)
Async XLA Ops:
  0.0 3.5 %copy-start.1 = (bf16[2,128,2048]{2,1,0:T(8,128)(2,1)S(1)}, bf16[2,128,2048]{2,1,0:T(8,128)(2,1)}, u32[]{:S(2)}) copy-start(bf16[2,128,2048]{2,1,0:T(8,128)(2,1)} %root_ref.5) | copy-start | bytes 3145732
  0.0 3.5 %copy-start = (bf16[2,2,128,2048]{3,2,1,0:T(8,128)(2,1)S(1)}, bf16[2,2,128,2048]{3,2,1,0:T(8,128)(2,1)}, u32[]{:S(2)}) copy-start(bf16[2,2,128,2048]{3,2,1,0:T(8,128)(2,1)} %noise_ref.5) | copy-start | bytes 6291460
  1.3 13.4 %collective-permute-start.4 = (f32[2,32,2048]{2,1,0:T(8,128)S(1)}, f32[2,32,2048]{2,1,0:T(8,128)S(1)}, u32[]{:S(2)}, u32[]{:S(2)}) collective-permute-start(f32[2,32,2048]{2,1,0:T(8,128)S(1)} %spectrum.5), channel_id=1, source_target_pairs={{0,2},{1,3},{2,0},{3,1},{4,6},{5,7},{6,4},{7,5},{8,10},{9,11},{10,... | collective-permute-start | bytes 1572872 | tf_op jit(solution)/shard_map/ppermute | solution.py:315
  5.2 22.9 %copy-start.6 = (bf16[256,256]{1,0:T(8,128)(2,1)S(1)}, bf16[256,256]{1,0:T(8,128)(2,1)}, u32[]{:S(2)}) copy-start(bf16[256,256]{1,0:T(8,128)(2,1)} %constant.23.lo_ref) | copy-start | bytes 393220
  5.3 22.9 %copy-start.7 = (bf16[256,256]{1,0:T(8,128)(2,1)S(1)}, bf16[256,256]{1,0:T(8,128)(2,1)}, u32[]{:S(2)}) copy-start(bf16[256,256]{1,0:T(8,128)(2,1)} %constant.20.hi_ref) | copy-start | bytes 393220
  5.3 22.9 %copy-start.8 = (f32[128,128]{1,0:T(8,128)S(1)}, f32[128,128]{1,0:T(8,128)}, u32[]{:S(2)}) copy-start(f32[128,128]{1,0:T(8,128)} %constant.18.clone.twist_ref) | copy-start | bytes 196612
  5.3 13.6 %collective-permute-start.3 = (f32[2,32,2048]{2,1,0:T(8,128)S(1)}, f32[2,32,2048]{2,1,0:T(8,128)S(1)}, u32[]{:S(2)}, u32[]{:S(2)}) collective-permute-start(f32[2,32,2048]{2,1,0:T(8,128)S(1)} %get-tuple-element.17), channel_id=1, source_target_pairs={{0,1},{1,0},{2,3},{3,2},{4,5},{5,4},{6,7},{7,6},{8,9},{9,8},{10,11... | collective-permute-start | bytes 1572872 | tf_op jit(solution)/shard_map/ppermute | solution.py:315
  6.3 21.8 %collective-permute-start.5 = (f32[2,32,2048]{2,1,0:T(8,128)S(1)}, f32[2,32,2048]{2,1,0:T(8,128)S(1)}, u32[]{:S(2)}, u32[]{:S(2)}) collective-permute-start(f32[2,32,2048]{2,1,0:T(8,128)S(1)} %get-tuple-element.18), channel_id=1, source_target_pairs={{0,3},{1,2},{2,1},{3,0},{4,7},{5,6},{6,5},{7,4},{8,11},{9,10},{10,... | collective-permute-start | bytes 1572872 | tf_op jit(solution)/shard_map/ppermute | solution.py:315
  10.2 0.8 copy-start.9
  11.0 31.9 %collective-permute-start = (f32[2,32,2048]{2,1,0:T(8,128)}, f32[2,32,2048]{2,1,0:T(8,128)S(1)}, u32[]{:S(2)}, u32[]{:S(2)}) collective-permute-start(f32[2,32,2048]{2,1,0:T(8,128)} %get-tuple-element.13), channel_id=1, source_target_pairs={{0,1},{1,0},{2,3},{3,2},{4,5},{5,4},{6,7},{7,6},{8,9},{9,8},{10,11... | collective-permute-start | bytes 1572872 | tf_op jit(solution)/shard_map/ppermute | solution.py:315
  11.4 31.5 %collective-permute-start.1 = (f32[2,32,2048]{2,1,0:T(8,128)}, f32[2,32,2048]{2,1,0:T(8,128)S(1)}, u32[]{:S(2)}, u32[]{:S(2)}) collective-permute-start(f32[2,32,2048]{2,1,0:T(8,128)} %get-tuple-element.14), channel_id=1, source_target_pairs={{0,2},{1,3},{2,0},{3,1},{4,6},{5,7},{6,4},{7,5},{8,10},{9,11},{10,... | collective-permute-start | bytes 1572872 | tf_op jit(solution)/shard_map/ppermute | solution.py:315
  14.7 49.9 %collective-permute-start.2 = (f32[2,32,2048]{2,1,0:T(8,128)}, f32[2,32,2048]{2,1,0:T(8,128)S(1)}, u32[]{:S(2)}, u32[]{:S(2)}) collective-permute-start(f32[2,32,2048]{2,1,0:T(8,128)} %get-tuple-element.15), channel_id=1, source_target_pairs={{0,3},{1,2},{2,1},{3,0},{4,7},{5,6},{6,5},{7,4},{8,11},{9,10},{10,... | collective-permute-start | bytes 1572872 | tf_op jit(solution)/shard_map/ppermute | solution.py:315
  32.2 32.4 %copy-start.10 = (f32[2,32,2048]{2,1,0:T(8,128)S(1)}, f32[2,32,2048]{2,1,0:T(8,128)}, u32[]{:S(2)}) copy-start(f32[2,32,2048]{2,1,0:T(8,128)} %copy-done.9) | copy-start | bytes 1572868
  32.2 45.5 %all-to-all-start.1 = ((f32[128,32,128]{2,1,0:T(8,128)}), f32[128,32,128]{2,1,0:T(8,128)}, u32[]{:S(2)}, u32[]{:S(2)}) async-start(f32[128,32,128]{2,1,0:T(8,128)} %columns.3), calls=%async_computation.1 | async-start | bytes 4194304 | tf_op jit(solution)/shard_map/all_to_all | solution.py:319
  68.0 1.3 %copy-start.2 = (f32[128,32,128]{2,1,0:T(8,128)}, f32[128,32,128]{2,1,0:T(8,128)S(1)}, u32[]{:S(2)}) copy-start(f32[128,32,128]{2,1,0:T(8,128)S(1)} %columns.2) | copy-start | bytes 6291460
  69.3 13.6 %copy-start.3 = (bf16[256,512]{1,0:T(8,128)(2,1)S(1)}, bf16[256,512]{1,0:T(8,128)(2,1)}, u32[]{:S(2)}) copy-start(bf16[256,512]{1,0:T(8,128)(2,1)} %constant.27.lo_ref) | copy-start | bytes 786436
  69.3 13.6 %copy-start.4 = (bf16[256,512]{1,0:T(8,128)(2,1)S(1)}, bf16[256,512]{1,0:T(8,128)(2,1)}, u32[]{:S(2)}) copy-start(bf16[256,512]{1,0:T(8,128)(2,1)} %constant.24.hi_ref) | copy-start | bytes 786436
  69.3 13.6 %copy-start.5 = (f32[32,8,128]{2,1,0:T(8,128)S(1)}, f32[32,8,128]{2,1,0:T(8,128)}, u32[]{:S(2)}) copy-start(f32[32,8,128]{2,1,0:T(8,128)} %constant.19.clone.twist_ref) | copy-start | bytes 393220
  77.7 34.4 %all-to-all-start = ((f32[128,32,128]{2,1,0:T(8,128)}), f32[128,32,128]{2,1,0:T(8,128)S(1)}, u32[]{:S(2)}, u32[]{:S(2)}) async-start(f32[128,32,128]{2,1,0:T(8,128)} %copy-done.2), calls=%async_computation | async-start | bytes 4194304 | tf_op jit(solution)/shard_map/all_to_all | solution.py:319
